TPU v7x, 32 devices: a whole 2x2x4 slice. The times are simulated.
32 devices in a mesh: parts: 2 (over x), aux: 4 (over y, core), occ: 4 (over z).
Axes of the slice: x: 2, y: 2, z: 4, core: 2. Of those that a mesh axis runs over, the one named last changes fastest.
Arguments:
- three_center: bfloat16 [20480, 4, 2, 2048], P(('parts', 'aux'), 'occ'), parts along dimension 0, may hold values from -1.5 to 1.5
- tile_mask: int32 [8, 2, 32], P(('parts', 'occ')), parts along dimension 0, may hold values 0 or 1
- pair_orbitals: int32 [8, 2], P(('parts', 'occ')), parts along dimension 0, may hold values from 0 to 639
- occ_energy: float32 [1280], P('parts'), parts along dimension 0, may hold values from -1.2 to -0.3
- vir_energy: float32 [4096], P('parts'), parts along dimension 0, may hold values from 0.2 to 4
Outputs:
- gamma: bfloat16 [20480, 4, 2048], P(('parts', 'aux'), 'occ'), parts along dimension 0
- vir_density: float32 [4096, 2048], P(('parts', 'aux'), 'occ'), parts along dimension 0
There are 2 independent parts, one for each index of `parts`. A program takes and returns all parts, laid end to end along the dimension named above; each array names one. Nothing has to cross between parts.
All inputs are finite; a program needn't handle non-finite values. No bound on the sum of `tile_mask` on one device may be relied on, other than what follows from the above.
Results may differ from a plain program's by a relative error of at most 0.014.
Values may be sent and summed in bfloat16 or wider, within the bound.
A program may use at most 192 MiB of HBM per device.

v0:
```python
import jax
import jax.numpy as jnp
from jax import lax
from jax.sharding import PartitionSpec as P


def body(three_center, tile_mask, pair_orbitals, occ_energy, vir_energy):
    nvirt = three_center.shape[3]
    slab = nvirt // lax.axis_size("aux")
    width = nvirt // tile_mask.shape[2]
    tile_keep = jnp.repeat(tile_mask, width, axis=2).astype(jnp.bfloat16)
    screened = three_center * tile_keep[None]
    first_orbital = screened[:, :, 0, :]
    second_orbital = screened[:, :, 1, :]
    orbital_range = jnp.arange(occ_energy.shape[0], dtype=jnp.int32)
    matches = pair_orbitals[:, :, None] == orbital_range[None, None, :]
    picked = jnp.sum(jnp.where(matches, occ_energy[None, None, :], 0.0), axis=2)
    shift = picked[:, 0] + picked[:, 1]
    offset = lax.axis_index("aux") * slab
    coulomb = lax.psum_scatter(
        jnp.einsum(
            "qpa,qpb->apb", first_orbital, second_orbital, preferred_element_type=jnp.float32
        ).astype(jnp.bfloat16),
        "aux",
        scatter_dimension=0,
        tiled=True,
    ).astype(jnp.float32)
    vir_rows = lax.dynamic_slice_in_dim(vir_energy, offset, slab, 0)
    denominator = shift[None, :, None] - vir_rows[:, None, None] - vir_energy[None, None, :]
    amplitude = (coulomb / denominator).astype(jnp.bfloat16)
    columns = lax.all_to_all(amplitude, "aux", split_axis=2, concat_axis=0, tiled=True)
    mirrored = jnp.transpose(columns, (2, 1, 0))
    tilde_part = (2.0 * amplitude.astype(jnp.float32) - mirrored.astype(jnp.float32)).astype(
        jnp.bfloat16
    )
    piece = lax.all_gather(tilde_part, "aux", axis=0, tiled=True)
    gamma_part = jnp.einsum(
        "qpb,apb->qpa", second_orbital, piece, preferred_element_type=jnp.float32
    )
    density_part = jnp.einsum("apc,bpc->ab", amplitude, piece, preferred_element_type=jnp.float32)
    vir_density = lax.psum_scatter(
        density_part.astype(jnp.bfloat16), "occ", scatter_dimension=1, tiled=True
    ).astype(jnp.float32)
    return (gamma_part.astype(jnp.bfloat16), vir_density)


def solution(mesh):
    in_specs = (
        P(("parts", "aux"), "occ", None, None),
        P(("parts", "occ"), None, None),
        P(("parts", "occ"), None),
        P("parts"),
        P("parts"),
    )
    out_specs = (P(("parts", "aux"), "occ", None), P(("parts", "aux"), "occ"))
    return jax.shard_map(body, mesh=mesh, in_specs=in_specs, out_specs=out_specs, check_vma=False)
```

profile of v0, /device:TPU:0, one launch (start us, length us, event | category | flops | bytes accessed | tf_op | source)
XLA Modules:
  0.0 341.1 jit_solution(18419097694668669605)
XLA Ops:
  7.2 0.0 reduce-scatter.3.cloned.1.call-start
  7.2 0.7 convert_bitcast_fusion.1
  7.9 0.1 broadcast_in_dim.14
  8.0 0.1 convert_element_type.69
  8.1 21.8 %copy_multiply_fusion = bf16[2560,1,2,2048]{3,0,2,1:T(8,128)(2,1)} fusion(bf16[2560,1,2,2048]{3,2,1,0:T(2,128)(2,1)} %param.5, bf16[2,2048]{1,0:T(2,128)(2,1)S(1)} %convert_element_type.69), kind=kLoop, calls=%fused_computation | loop fusion | flops 10485760 | bytes 41951232 | tf_op jit(solution)/shard_map/mul | solution.py:12
  29.9 28.8 %convert_bitcast_fusion = bf16[2048,1,2048]{0,2,1:T(8,128)(2,1)} fusion(bf16[2560,1,2,2048]{3,0,2,1:T(8,128)(2,1)} %copy_multiply_fusion), kind=kOutput, calls=%fused_computation.9 | convolution fusion | flops 21479030784 | bytes 29360128 | tf_op jit(solution)/shard_map/qpa,qpb->apb/dot_general | solution.py:21
  58.7 0.0 reduce-scatter.3.cloned.1.call-update
  58.7 0.2 all-gather.2.cloned.1.call-start
  58.9 0.4 copy-done.3
  59.3 0.2 fusion.10
  59.5 0.6 fusion.11
  61.5 0.1 dynamic-slice_subtract_fusion
  61.5 71.7 %reduce-scatter.3.cloned.1.call-done = bf16[512,1,2048]{0,2,1:T(8,128)(2,1)} async-done(((bf16[2048,1,2048]{0,2,1:T(8,128)(2,1)}), bf16[512,1,2048]{0,2,1:T(8,128)(2,1)}) %reduce-scatter.3.cloned.1.call-update) | async-done | bytes 2097168 | tf_op jit(solution)/shard_map/reduce_scatter | solution.py:20
  133.3 2.3 divide_convert_fusion
  135.6 1.3 copy-done
  136.9 18.5 %copy.22 = bf16[512,1,2048]{0,1,2:T(2,128)(2,1)} copy(bf16[512,1,2048]{0,2,1:T(8,128)(2,1)S(1)} %divide_convert_fusion) | data formatting | bytes 4194304 | tf_op jit(solution)/shard_map/convert_element_type | solution.py:30
  155.4 0.5 broadcast.100
  155.9 14.1 %reduce.1 = bf16[2048,512]{1,0:T(8,128)(2,1)S(1)} reduce(bf16[2048,1,512]{2,1,0:T(2,128)(2,1)} %bitcast.48, bf16[]{:T(256)} %broadcast.100), dimensions={1}, to_apply=%bitcast.47.reduce_sub_computation | reduce | bytes 4194306
  170.0 2.8 reshape.170
  172.7 29.3 %all_to_all.4 = bf16[4,2,131072]{2,1,0:T(2,128)(2,1)S(1)} all-to-all(bf16[4,2,131072]{2,1,0:T(2,128)(2,1)} %reshape.170), channel_id=1, replica_groups=mesh['parts'=2,'aux'=4,'occ'=4] {'aux'}, dimensions={0} | all-to-all | bytes 4194304 | tf_op jit(solution)/shard_map/all_to_all | solution.py:31
  202.0 3.3 reshape.171
  205.3 11.0 %copy.18 = f32[512,1,4,512]{3,0,2,1:T(8,128)} copy(bf16[512,1,4,512]{0,1,3,2:T(2,128)(2,1)} %bitcast.49) | data formatting | bytes 6291456 | tf_op jit(solution)/shard_map/convert_element_type | solution.py:33
  216.3 4.4 %fusion.5 = bf16[512,1,2048]{0,2,1:T(8,128)(2,1)} fusion(f32[512,1,4,512]{3,0,2,1:T(8,128)} %copy.18, f32[2048]{0:T(1024)S(1)} %copy-done.2, f32[512]{0:T(512)S(1)} %dynamic-slice_subtract_fusion, bf16[512,1,2048]{0,2,1:T(8,128)(2,1)} %reduce-scatter.3.cloned.1.call-done), kind=kLoop, calls=%fused_computation.11 | loop fusion | flops 8388608 | bytes 8398848 | tf_op jit(solution)/shard_map/convert_element_type | solution.py:33
  220.8 0.0 all-gather.2.cloned.1.call-update
  220.8 0.3 reduce-scatter.5.cloned.1.call-start
  221.1 58.2 %all-gather.2.cloned.1.call-done = bf16[2048,1,2048]{0,2,1:T(8,128)(2,1)} async-done(((bf16[512,1,2048]{0,2,1:T(8,128)(2,1)}), bf16[2048,1,2048]{0,2,1:T(8,128)(2,1)}) %all-gather.2.cloned.1.call-update) | async-done | bytes 8388624 | tf_op jit(solution)/shard_map/all_gather | solution.py:36
  279.2 9.1 %fusion.6 = bf16[512,2048]{1,0:T(8,128)(2,1)} fusion(bf16[2048,1,2048]{0,2,1:T(8,128)(2,1)} %all-gather.2.cloned.1.call-done, bf16[512,1,2048]{0,2,1:T(8,128)(2,1)S(1)} %copy-done.1), kind=kOutput, calls=%fused_computation.13 | convolution fusion | flops 4296015872 | bytes 12582912 | tf_op jit(solution)/shard_map/apc,bpc->ab/dot_general | solution.py:40
  288.4 0.0 reduce-scatter.5.cloned.1.call-update
  288.4 28.6 %fusion.1 = bf16[2560,1,2048]{0,2,1:T(8,128)(2,1)} fusion(bf16[2560,1,2,2048]{3,0,2,1:T(8,128)(2,1)} %copy_multiply_fusion, bf16[2048,1,2048]{0,2,1:T(8,128)(2,1)} %all-gather.2.cloned.1.call-done), kind=kOutput, calls=%fused_computation.5 | convolution fusion | flops 21480079360 | bytes 29360128 | tf_op jit(solution)/shard_map/qpb,apb->qpa/dot_general | solution.py:37
  317.0 14.4 %copy.19 = bf16[2560,1,2048]{2,0,1:T(8,128)(2,1)} copy(bf16[2560,1,2048]{0,2,1:T(8,128)(2,1)} %fusion.1) | data formatting | bytes 20971520
  331.5 1.0 reduce-scatter.5.cloned.1.call-done
  332.4 2.1 convert_element_type.86
  (8 shorter events, 0.0 us)
Async XLA Ops:
  7.2 126.1 %reduce-scatter.3.cloned.1.call-start = ((), (), s32[]{:S(2)}) async-start(), calls=%async_computation.3 | async-start | bytes 10485760 | tf_op jit(solution)/shard_map/reduce_scatter | solution.py:20
  58.7 0.7 copy-start.3
  58.7 0.7 copy-start.4
  58.7 2.8 copy-start.2
  58.7 220.5 %all-gather.2.cloned.1.call-start = ((), (), s32[]{:S(2)}) async-start(), calls=%async_computation.4 | async-start | bytes 10485760 | tf_op jit(solution)/shard_map/all_gather | solution.py:36
  135.6 1.3 copy-start
  216.3 62.9 %copy-start.1 = (bf16[512,1,2048]{0,2,1:T(8,128)(2,1)S(1)}, bf16[512,1,2048]{0,2,1:T(8,128)(2,1)}, u32[]{:S(2)}) copy-start(bf16[512,1,2048]{0,2,1:T(8,128)(2,1)} %copy-done) | copy-start | bytes 6291460
  220.8 111.6 %reduce-scatter.5.cloned.1.call-start = ((), (), s32[]{:S(2)}) async-start(), calls=%async_computation.5 | async-start | bytes 2621440 | tf_op jit(solution)/shard_map/reduce_scatter | solution.py:41
Sparse Core Ops, SparseCore 0:
  58.8 74.3 reduce-scatter.2
  220.9 58.2 all-gather.1
  288.5 43.8 reduce-scatter.4
where the time goes:
time: 342 us; the launch traced here: 341 us
  waiting for transfers between devices  131 us (38%)
  matrix products  66.5 us (19%)
  local copies, waits for them, and re-layouts  53 us (15%)
  other arithmetic  45.8 us (13%)
  blocking collectives  29.3 us (9%)
  between operations  15.1 us (4%)
    reduce_scatter x1, waiting for transfers between devices, body(): lax.psum_scatter(jnp.einsum('qpa,qpb->apb', first_orbital, second_orbital...  71.7 us
    all_gather x1, waiting for transfers between devices, body(): piece = lax.all_gather(tilde_part, 'aux', axis=0, tiled=True)  58.2 us
    all_to_all x1, blocking collectives, body(): lax.all_to_all(amplitude, 'aux', split_axis=2, concat_axis=0, tiled=True)  29.3 us
    dot_general x1, matrix products, body(): jnp.einsum('qpa,qpb->apb', first_orbital, second_orbital, preferred_eleme...  28.8 us
    dot_general x1, matrix products, body(): jnp.einsum('qpb,apb->qpa', second_orbital, piece, preferred_element_type=...  28.6 us
    unnamed x14, local copies, waits for them, and re-layouts  22.7 us
    mul x1, other arithmetic, body(): screened = three_center * tile_keep[None]  21.8 us
    convert_element_type x1, local copies, waits for them, and re-layouts, body(): amplitude = (coulomb / denominator).astype(jnp.bfloat16)  18.5 us
  transfers between devices with their start and end apart: 3, of which 3 were waited for; matrix products, arithmetic and copies ran while one was open for 13% of the time, Pallas kernels for 0%

commit v1 on v0

--- a/solution.py
+++ b/solution.py
@@ -4,7 +4,14 @@
 from jax.sharding import PartitionSpec as P
 
 
-def body(three_center, tile_mask, pair_orbitals, occ_energy, vir_energy):
+def pick_shift(pair_orbitals, occ_energy):
+    orbital_range = jnp.arange(occ_energy.shape[0], dtype=jnp.int32)
+    matches = pair_orbitals[:, :, None] == orbital_range[None, None, :]
+    picked = jnp.sum(jnp.where(matches, occ_energy[None, None, :], 0.0), axis=2)
+    return picked[:, 0] + picked[:, 1]
+
+
+def general_body(three_center, tile_mask, pair_orbitals, occ_energy, vir_energy):
     nvirt = three_center.shape[3]
     slab = nvirt // lax.axis_size("aux")
     width = nvirt // tile_mask.shape[2]
@@ -12,10 +19,7 @@
     screened = three_center * tile_keep[None]
     first_orbital = screened[:, :, 0, :]
     second_orbital = screened[:, :, 1, :]
-    orbital_range = jnp.arange(occ_energy.shape[0], dtype=jnp.int32)
-    matches = pair_orbitals[:, :, None] == orbital_range[None, None, :]
-    picked = jnp.sum(jnp.where(matches, occ_energy[None, None, :], 0.0), axis=2)
-    shift = picked[:, 0] + picked[:, 1]
+    shift = pick_shift(pair_orbitals, occ_energy)
     offset = lax.axis_index("aux") * slab
     coulomb = lax.psum_scatter(
         jnp.einsum(
@@ -44,6 +48,64 @@
     return (gamma_part.astype(jnp.bfloat16), vir_density)
 
 
+SIBLING = [(0, 1), (1, 0), (2, 3), (3, 2)]
+ACROSS = [(0, 2), (2, 0), (1, 3), (3, 1)]
+CHUNKS = 4
+
+
+def body(three_center, tile_mask, pair_orbitals, occ_energy, vir_energy):
+    nvirt = three_center.shape[3]
+    if lax.axis_size("aux") != 4 or three_center.shape[1] != 1 or nvirt % (CHUNKS * 512):
+        return general_body(three_center, tile_mask, pair_orbitals, occ_energy, vir_energy)
+    slab = nvirt // 4
+    width = nvirt // tile_mask.shape[2]
+    keep = jnp.repeat(tile_mask[0], width, axis=1).astype(jnp.float32)
+    first = three_center[:, 0, 0, :]
+    second = three_center[:, 0, 1, :]
+    shift = pick_shift(pair_orbitals, occ_energy)[0]
+    me = lax.axis_index("aux")
+    core = lax.rem(me, 2)
+    rows = nvirt // CHUNKS
+    half = rows // 2
+    amplitude = jnp.zeros((nvirt, nvirt), jnp.bfloat16)
+    for k in range(CHUNKS):
+        part = lax.dot_general(
+            first[:, k * rows : (k + 1) * rows],
+            second,
+            (((0,), (0,)), ((), ())),
+            preferred_element_type=jnp.float32,
+        ).astype(jnp.bfloat16)
+        mine = lax.dynamic_slice_in_dim(part, core * half, half, 0)
+        other = lax.dynamic_slice_in_dim(part, (1 - core) * half, half, 0)
+        got = lax.ppermute(other, "aux", SIBLING)
+        chip = (mine.astype(jnp.float32) + got.astype(jnp.float32)).astype(jnp.bfloat16)
+        far = lax.ppermute(chip, "aux", ACROSS)
+        total = chip.astype(jnp.float32) + far.astype(jnp.float32)
+        start = k * rows + core * half
+        vir_rows = lax.dynamic_slice_in_dim(vir_energy, start, half, 0)
+        keep_rows = lax.dynamic_slice_in_dim(keep[0], start, half, 0)
+        denominator = shift - vir_rows[:, None] - vir_energy[None, :]
+        amp = (total / denominator * keep_rows[:, None] * keep[1][None, :]).astype(jnp.bfloat16)
+        amp_other = lax.ppermute(amp, "aux", SIBLING)
+        amplitude = lax.dynamic_update_slice_in_dim(amplitude, amp, start, 0)
+        amplitude = lax.dynamic_update_slice_in_dim(
+            amplitude, amp_other, k * rows + (1 - core) * half, 0
+        )
+    wide = amplitude.astype(jnp.float32)
+    tilde = ((2.0 * wide - wide.T) * keep[1][None, :]).astype(jnp.bfloat16)
+    own = lax.dynamic_slice_in_dim(amplitude, me * slab, slab, 0)
+    density_part = lax.dot_general(
+        own, tilde, (((1,), (1,)), ((), ())), preferred_element_type=jnp.float32
+    )
+    vir_density = lax.psum_scatter(
+        density_part.astype(jnp.bfloat16), "occ", scatter_dimension=1, tiled=True
+    ).astype(jnp.float32)
+    gamma = lax.dot_general(
+        second, tilde, (((1,), (1,)), ((), ())), preferred_element_type=jnp.float32
+    ).astype(jnp.bfloat16)
+    return (gamma[:, None, :], vir_density)
+
+
 def solution(mesh):
     in_specs = (
         P(("parts", "aux"), "occ", None, None),

time: 342 us -> 327 us (0.956)
  local copies, waits for them, and re-layouts: 53 us -> 136 us
  waiting for transfers between devices: 131 us -> 82.2 us
  blocking collectives: 29.3 us -> 0 us
  other arithmetic: 45.8 us -> 25.7 us
  matrix products: 66.5 us -> 59.1 us
  starting transfers between devices: 0.52 us -> 7.42 us
    ppermute x0 -> x12, waiting for transfers between devices: none -> 79.7 us  [the longest x4 79.7 us: body(): far = lax.ppermute(chip, 'aux', ACROSS)]
    reduce_scatter x1 -> x0, waiting for transfers between devices: 71.7 us -> none  [body(): lax.psum_scatter(jnp.einsum('qpa,qpb->apb', first_orbital, second_orbital...]
    all_gather x1 -> x0, waiting for transfers between devices: 58.2 us -> none  [body(): piece = lax.all_gather(tilde_part, 'aux', axis=0, tiled=True)]
    slice x1 -> x4, local copies, waits for them, and re-layouts: 0.59 us -> 41.2 us  [the longest x1 40.5 us: body(): first = three_center[:, 0, 0, :]]
    all_to_all x1 -> x0, blocking collectives: 29.3 us -> none  [body(): lax.all_to_all(amplitude, 'aux', split_axis=2, concat_axis=0, tiled=True)]
    squeeze x0 -> x1, local copies, waits for them, and re-layouts: none -> 27.2 us  [body(): second = three_center[:, 0, 1, :]]
    mul x1 -> x0, other arithmetic: 21.8 us -> none  [body(): screened = three_center * tile_keep[None]]
    convert_element_type x3 -> x7, other arithmetic: 7.46 us -> 23.3 us  [the longest x1 9.25 us: body(): tilde = ((2.0 * wide - wide.T) * keep[1][None, :]).astype(jnp.bfloat16)]
  transfers between devices with their start and end apart: 3 -> 13, of which waited for: 3 -> 5; matrix products, arithmetic and copies ran while one was open for 13% -> 31% of each run, Pallas kernels for 0% -> 0%
where the time goes in v1:
time: 327 us; the launch traced here: 326 us
  local copies, waits for them, and re-layouts  136 us (42%)
  waiting for transfers between devices  82.2 us (25%)
  matrix products  59.1 us (18%)
  other arithmetic  25.7 us (8%)
  between operations  15.6 us (5%)
  starting transfers between devices  7.42 us (2%)
    ppermute x4, waiting for transfers between devices, body(): far = lax.ppermute(chip, 'aux', ACROSS)  79.7 us
    slice x1, local copies, waits for them, and re-layouts, body(): first = three_center[:, 0, 0, :]  40.5 us
    dot_general x1, matrix products, body(): lax.dot_general(second, tilde, (((1,), (1,)), ((), ())), preferred_elemen...  28.5 us
    squeeze x1, local copies, waits for them, and re-layouts, body(): second = three_center[:, 0, 1, :]  27.2 us
    dot_general x4, matrix products, body(): lax.dot_general(first[:, k * rows:(k + 1) * rows], second, (((0,), (0,)),...  23.2 us
    unnamed x23, local copies, waits for them, and re-layouts  20 us
    convert_element_type x1, local copies, waits for them, and re-layouts, body(): wide = amplitude.astype(jnp.float32)  13.1 us
    convert_element_type x1, other arithmetic, body(): tilde = ((2.0 * wide - wide.T) * keep[1][None, :]).astype(jnp.bfloat16)  9.25 us
  transfers between devices with their start and end apart: 13, of which 5 were waited for; matrix products, arithmetic and copies ran while one was open for 31% of the time, Pallas kernels for 0%

profile of v1, /device:TPU:0, one launch (start us, length us, event | category | flops | bytes accessed | tf_op | source)
XLA Modules:
  0.0 325.8 jit_solution(13818783387219906819)
XLA Ops:
  7.2 40.5 %fusion.10 = (bf16[2560,1,1,2048]{3,2,1,0:T(2,128)(2,1)}, bf16[2560,1,1,2048]{3,2,1,0:T(2,128)(2,1)}) fusion(bf16[2560,1,2,2048]{3,2,1,0:T(2,128)(2,1)} %param.5), kind=kLoop, calls=%fused_computation.50 | loop fusion | bytes 41943040 | tf_op jit(solution)/shard_map/slice | solution.py:63
  47.7 27.2 %copy_bitcast_fusion = (bf16[2560,2048]{1,0:T(8,128)(2,1)S(1)}, bf16[2560,2048]{1,0:T(8,128)(2,1)S(1)}) fusion(bf16[2560,1,1,2048]{3,2,1,0:T(2,128)(2,1)} %get-tuple-element.9, bf16[2560,1,1,2048]{3,2,1,0:T(2,128)(2,1)} %get-tuple-element.8), kind=kLoop, calls=%fused_computation.4 | loop fusion | bytes 41943040 | tf_op jit(solution)/shard_map/squeeze | solution.py:64
  75.0 5.8 %convolution_convert_fusion.5 = bf16[512,2048]{1,0:T(8,128)(2,1)S(1)} fusion(bf16[2560,2048]{1,0:T(8,128)(2,1)S(1)} %get-tuple-element.26, bf16[2560,2048]{1,0:T(8,128)(2,1)S(1)} %get-tuple-element.27), kind=kOutput, calls=%fused_computation.11 | convolution fusion | flops 5369757696 | bytes 15204352 | tf_op jit(solution)/shard_map/dot_general | solution.py:72
  81.5 5.8 %convolution_convert_fusion.3 = bf16[512,2048]{1,0:T(8,128)(2,1)S(1)} fusion(bf16[2560,2048]{1,0:T(8,128)(2,1)S(1)} %get-tuple-element.26, bf16[2560,2048]{1,0:T(8,128)(2,1)S(1)} %get-tuple-element.27), kind=kOutput, calls=%fused_computation.9 | convolution fusion | flops 5369757696 | bytes 15204352 | tf_op jit(solution)/shard_map/dot_general | solution.py:72
  89.0 5.8 %convolution_convert_fusion.4 = bf16[512,2048]{1,0:T(8,128)(2,1)S(1)} fusion(bf16[2560,2048]{1,0:T(8,128)(2,1)S(1)} %get-tuple-element.26, bf16[2560,2048]{1,0:T(8,128)(2,1)S(1)} %get-tuple-element.27), kind=kOutput, calls=%fused_computation.10 | convolution fusion | flops 5369757696 | bytes 15204352 | tf_op jit(solution)/shard_map/dot_general | solution.py:72
  97.0 5.8 %convolution_convert_fusion.2 = bf16[512,2048]{1,0:T(8,128)(2,1)S(1)} fusion(bf16[2560,2048]{1,0:T(8,128)(2,1)S(1)} %get-tuple-element.26, bf16[2560,2048]{1,0:T(8,128)(2,1)S(1)} %get-tuple-element.27), kind=kOutput, calls=%fused_computation.8 | convolution fusion | flops 5369757696 | bytes 15204352 | tf_op jit(solution)/shard_map/dot_general | solution.py:72
  105.2 1.8 add_convert_fusion.3
  107.0 3.0 collective-permute-start.1
  110.0 1.9 add_convert_fusion.1
  112.1 1.9 add_convert_fusion.2
  114.0 2.1 collective-permute-start.4
  116.1 2.6 add_convert_fusion
  121.3 12.9 %collective-permute-done.1 = bf16[256,2048]{1,0:T(8,128)(2,1)} collective-permute-done((bf16[256,2048]{1,0:T(8,128)(2,1)S(1)}, bf16[256,2048]{1,0:T(8,128)(2,1)}, u32[]{:S(2)}, u32[]{:S(2)}) %collective-permute-start.1) | collective-permute-done | bytes 1048608 | tf_op jit(solution)/shard_map/ppermute | solution.py:82
  134.1 22.5 %collective-permute-done.7 = bf16[256,2048]{1,0:T(8,128)(2,1)} collective-permute-done((bf16[256,2048]{1,0:T(8,128)(2,1)S(1)}, bf16[256,2048]{1,0:T(8,128)(2,1)}, u32[]{:S(2)}, u32[]{:S(2)}) %collective-permute-start.7) | collective-permute-done | bytes 1048608 | tf_op jit(solution)/shard_map/ppermute | solution.py:82
  156.6 22.5 %collective-permute-done.4 = bf16[256,2048]{1,0:T(8,128)(2,1)} collective-permute-done((bf16[256,2048]{1,0:T(8,128)(2,1)S(1)}, bf16[256,2048]{1,0:T(8,128)(2,1)}, u32[]{:S(2)}, u32[]{:S(2)}) %collective-permute-start.4) | collective-permute-done | bytes 1048608 | tf_op jit(solution)/shard_map/ppermute | solution.py:82
  179.1 21.9 %collective-permute-done.10 = bf16[256,2048]{1,0:T(8,128)(2,1)} collective-permute-done((bf16[256,2048]{1,0:T(8,128)(2,1)}, bf16[256,2048]{1,0:T(8,128)(2,1)}, u32[]{:S(2)}, u32[]{:S(2)}) %collective-permute-start.10) | collective-permute-done | bytes 1048608 | tf_op jit(solution)/shard_map/ppermute | solution.py:82
  200.9 5.8 %multiply_convert_fusion = (bf16[256,2048]{1,0:T(8,128)(2,1)}, bf16[256,2048]{1,0:T(8,128)(2,1)}, bf16[256,2048]{1,0:T(8,128)(2,1)}, bf16[256,2048]{1,0:T(8,128)(2,1)}) fusion(bf16[256,2048]{1,0:T(8,128)(2,1)} %collective-permute-done.10, bf16[256,2048]{1,0:T(8,128)(2,1)} %add_convert_fusion, f32[256]{0:T(256)S(1)} %bitcast.33, ...), kind=kLoop, calls=%fused_computation.17 | loop fusion | flops 16777216 | bytes 12607488 | tf_op jit(solution)/shard_map/convert_element_type | solution.py:88
  207.3 2.3 copy.33
  211.1 1.5 copy.37
  214.6 4.5 %broadcast_in_dim.20 = bf16[2048,2048]{0,1:T(8,128)(2,1)} broadcast(bf16[]{:T(256)} %constant.26.clone.1), dimensions={} | broadcast | bytes 8388610 | tf_op jit(solution)/shard_map/broadcast_in_dim | solution.py:70
  220.2 2.3 copy.34
  222.5 2.4 constant_dynamic-update-slice_fusion.6
  226.0 2.3 copy.36
  229.8 2.4 constant_dynamic-update-slice_fusion.4
  238.3 13.1 %copy.41 = f32[2048,2048]{1,0:T(8,128)} copy(bf16[2048,2048]{0,1:T(8,128)(2,1)} %constant_dynamic-update-slice_fusion) | data formatting | bytes 25165824 | tf_op jit(solution)/shard_map/convert_element_type | solution.py:94
  251.3 9.2 %fusion.1 = bf16[2048,2048]{0,1:T(8,128)(2,1)S(1)} fusion(f32[2048,2048]{1,0:T(8,128)} %copy.41, f32[2048]{0:T(1024)S(1)} %mul.110, bf16[2048,2048]{0,1:T(8,128)(2,1)} %constant_dynamic-update-slice_fusion), kind=kLoop, calls=%fused_computation.2 | loop fusion | flops 20971520 | bytes 33562624 | tf_op jit(solution)/shard_map/convert_element_type | solution.py:95
  260.6 3.3 %copy-done.1 = bf16[2048,2048]{0,1:T(8,128)(2,1)} copy-done((bf16[2048,2048]{0,1:T(8,128)(2,1)}, bf16[2048,2048]{0,1:T(8,128)(2,1)S(1)}, u32[]{:S(2)}) %copy-start.1) | copy-done | bytes 8388632
  263.9 7.4 %convolution_convert_fusion.1 = bf16[512,2048]{1,0:T(8,128)(2,1)} fusion(bf16[2048,2048]{0,1:T(8,128)(2,1)S(1)} %fusion.1, bf16[2048,2048]{0,1:T(8,128)(2,1)} %constant_dynamic-update-slice_fusion, s32[]{:T(128)S(6)} %select_n.70), kind=kOutput, calls=%fused_computation.7 | convolution fusion | flops 4296015872 | bytes 12582916 | tf_op jit(solution)/shard_map/dot_general | solution.py:97
  271.3 28.5 %fusion.2 = bf16[2560,1,2048]{0,2,1:T(8,128)(2,1)} fusion(bf16[2048,2048]{0,1:T(8,128)(2,1)} %copy-done.1, bf16[2560,2048]{1,0:T(8,128)(2,1)} %copy-done), kind=kOutput, calls=%fused_computation.6 | convolution fusion | flops 21480079360 | bytes 29360128 | tf_op jit(solution)/shard_map/dot_general | solution.py:103
  299.9 14.4 %copy.43 = bf16[2560,1,2048]{2,0,1:T(8,128)(2,1)} copy(bf16[2560,1,2048]{0,2,1:T(8,128)(2,1)} %fusion.2) | data formatting | bytes 20971520
  314.3 2.5 reduce-scatter.2.cloned.1.call-done
  316.8 2.1 convert_element_type.142
  (65 shorter events, 22.3 us)
Async XLA Ops:
  7.2 309.6 %reduce-scatter.2.cloned.1.call-start = ((), (), s32[]{:S(2)}) async-start(), calls=%async_computation.1 | async-start | bytes 2621440 | tf_op jit(solution)/shard_map/reduce_scatter | solution.py:100
  75.0 22.0 %copy-start = (bf16[2560,2048]{1,0:T(8,128)(2,1)}, bf16[2560,2048]{1,0:T(8,128)(2,1)S(1)}, u32[]{:S(2)}) copy-start(bf16[2560,2048]{1,0:T(8,128)(2,1)S(1)} %get-tuple-element.26) | copy-start | bytes 31457284
  80.9 24.3 %collective-permute-start = (bf16[256,2048]{1,0:T(8,128)(2,1)S(1)}, bf16[256,2048]{1,0:T(8,128)(2,1)}, u32[]{:S(2)}, u32[]{:S(2)}) collective-permute-start(bf16[256,2048]{1,0:T(8,128)(2,1)S(1)} %constant_dynamic-slice_fusion.7), channel_id=1, source_target_pairs={{0,4},{4,0},{8,12},{12,8},{1,5},{5,1},{9,13},{13,9},{2,6},{6,2},{1... | collective-permute-start | bytes 3145736 | tf_op jit(solution)/shard_map/ppermute | solution.py:80
  87.3 1.7 copy-start.6
  89.0 21.1 %collective-permute-start.6 = (bf16[256,2048]{1,0:T(8,128)(2,1)}, bf16[256,2048]{1,0:T(8,128)(2,1)}, u32[]{:S(2)}, u32[]{:S(2)}) collective-permute-start(bf16[256,2048]{1,0:T(8,128)(2,1)} %constant_dynamic-slice_fusion.3), channel_id=1, source_target_pairs={{0,4},{4,0},{8,12},{12,8},{1,5},{5,1},{9,13},{13,9},{2,6},{6,2},{1... | collective-permute-start | bytes 3145736 | tf_op jit(solution)/shard_map/ppermute | solution.py:80
  94.8 1.7 copy-start.5
  96.5 15.6 %collective-permute-start.3 = (bf16[256,2048]{1,0:T(8,128)(2,1)}, bf16[256,2048]{1,0:T(8,128)(2,1)}, u32[]{:S(2)}, u32[]{:S(2)}) collective-permute-start(bf16[256,2048]{1,0:T(8,128)(2,1)} %constant_dynamic-slice_fusion.5), channel_id=1, source_target_pairs={{0,4},{4,0},{8,12},{12,8},{1,5},{5,1},{9,13},{13,9},{2,6},{6,2},{1... | collective-permute-start | bytes 3145736 | tf_op jit(solution)/shard_map/ppermute | solution.py:80
  102.8 1.3 copy-start.3
  104.1 14.6 %copy-start.9 = (s32[1,2,32]{2,1,0:T(2,128)S(1)}, s32[1,2,32]{2,1,0:T(2,128)}, u32[]{:S(2)}) copy-start(s32[1,2,32]{2,1,0:T(2,128)} %param.6) | copy-start | bytes 772
  104.1 14.9 %copy-start.8 = (f32[640]{0:T(1024)S(1)}, f32[640]{0:T(1024)}, u32[]{:S(2)}) copy-start(f32[640]{0:T(1024)} %param.8) | copy-start | bytes 7684
  104.1 14.9 %copy-start.10 = (s32[1,2]{1,0:T(1,128)S(1)}, s32[1,2]{1,0:T(1,128)}, u32[]{:S(2)}) copy-start(s32[1,2]{1,0:T(1,128)} %param.7) | copy-start | bytes 28
  104.1 17.1 %copy-start.7 = (f32[2048]{0:T(1024)S(1)}, f32[2048]{0:T(1024)}, u32[]{:S(2)}) copy-start(f32[2048]{0:T(1024)} %param.9) | copy-start | bytes 24580
  105.2 10.9 %collective-permute-start.9 = (bf16[256,2048]{1,0:T(8,128)(2,1)}, bf16[256,2048]{1,0:T(8,128)(2,1)}, u32[]{:S(2)}, u32[]{:S(2)}) collective-permute-start(bf16[256,2048]{1,0:T(8,128)(2,1)} %constant_dynamic-slice_fusion.1), channel_id=1, source_target_pairs={{0,4},{4,0},{8,12},{12,8},{1,5},{5,1},{9,13},{13,9},{2,6},{6,2},{1... | collective-permute-start | bytes 3145736 | tf_op jit(solution)/shard_map/ppermute | solution.py:80
  105.2 10.8 %copy-start.4 = (bf16[512,2048]{1,0:T(8,128)(2,1)S(1)}, bf16[512,2048]{1,0:T(8,128)(2,1)}, u32[]{:S(2)}) copy-start(bf16[512,2048]{1,0:T(8,128)(2,1)} %copy-done.3) | copy-start | bytes 6291460
  107.0 27.1 %collective-permute-start.1 = (bf16[256,2048]{1,0:T(8,128)(2,1)S(1)}, bf16[256,2048]{1,0:T(8,128)(2,1)}, u32[]{:S(2)}, u32[]{:S(2)}) collective-permute-start(bf16[256,2048]{1,0:T(8,128)(2,1)S(1)} %add_convert_fusion.3), channel_id=1, source_target_pairs={{0,8},{8,0},{4,12},{12,4},{1,9},{9,1},{5,13},{13,5},{2,10},{10,2},... | collective-permute-start | bytes 3145736 | tf_op jit(solution)/shard_map/ppermute | solution.py:82
  112.0 44.6 %collective-permute-start.7 = (bf16[256,2048]{1,0:T(8,128)(2,1)S(1)}, bf16[256,2048]{1,0:T(8,128)(2,1)}, u32[]{:S(2)}, u32[]{:S(2)}) collective-permute-start(bf16[256,2048]{1,0:T(8,128)(2,1)S(1)} %add_convert_fusion.1), channel_id=1, source_target_pairs={{0,8},{8,0},{4,12},{12,4},{1,9},{9,1},{5,13},{13,5},{2,10},{10,2},... | collective-permute-start | bytes 3145736 | tf_op jit(solution)/shard_map/ppermute | solution.py:82
  114.0 65.0 %collective-permute-start.4 = (bf16[256,2048]{1,0:T(8,128)(2,1)S(1)}, bf16[256,2048]{1,0:T(8,128)(2,1)}, u32[]{:S(2)}, u32[]{:S(2)}) collective-permute-start(bf16[256,2048]{1,0:T(8,128)(2,1)S(1)} %add_convert_fusion.2), channel_id=1, source_target_pairs={{0,8},{8,0},{4,12},{12,4},{1,9},{9,1},{5,13},{13,5},{2,10},{10,2},... | collective-permute-start | bytes 3145736 | tf_op jit(solution)/shard_map/ppermute | solution.py:82
  118.7 82.2 %collective-permute-start.10 = (bf16[256,2048]{1,0:T(8,128)(2,1)}, bf16[256,2048]{1,0:T(8,128)(2,1)}, u32[]{:S(2)}, u32[]{:S(2)}) collective-permute-start(bf16[256,2048]{1,0:T(8,128)(2,1)} %add_convert_fusion), channel_id=1, source_target_pairs={{0,8},{8,0},{4,12},{12,4},{1,9},{9,1},{5,13},{13,5},{2,10},{10,2},... | collective-permute-start | bytes 3145736 | tf_op jit(solution)/shard_map/ppermute | solution.py:82
  206.7 13.5 %collective-permute-start.2 = (bf16[256,2048]{1,0:T(8,128)(2,1)}, bf16[256,2048]{1,0:T(8,128)(2,1)}, u32[]{:S(2)}, u32[]{:S(2)}) collective-permute-start(bf16[256,2048]{1,0:T(8,128)(2,1)} %get-tuple-element.13), channel_id=1, source_target_pairs={{0,4},{4,0},{8,12},{12,8},{1,5},{5,1},{9,13},{13,9},{2,6},{6,2},{1... | collective-permute-start | bytes 3145736 | tf_op jit(solution)/shard_map/ppermute | solution.py:89
  206.7 19.3 %collective-permute-start.5 = (bf16[256,2048]{1,0:T(8,128)(2,1)}, bf16[256,2048]{1,0:T(8,128)(2,1)}, u32[]{:S(2)}, u32[]{:S(2)}) collective-permute-start(bf16[256,2048]{1,0:T(8,128)(2,1)} %get-tuple-element.11), channel_id=1, source_target_pairs={{0,4},{4,0},{8,12},{12,8},{1,5},{5,1},{9,13},{13,9},{2,6},{6,2},{1... | collective-permute-start | bytes 3145736 | tf_op jit(solution)/shard_map/ppermute | solution.py:89
  207.2 21.1 %collective-permute-start.8 = (bf16[256,2048]{1,0:T(8,128)(2,1)}, bf16[256,2048]{1,0:T(8,128)(2,1)}, u32[]{:S(2)}, u32[]{:S(2)}) collective-permute-start(bf16[256,2048]{1,0:T(8,128)(2,1)} %get-tuple-element.12), channel_id=1, source_target_pairs={{0,4},{4,0},{8,12},{12,8},{1,5},{5,1},{9,13},{13,9},{2,6},{6,2},{1... | collective-permute-start | bytes 3145736 | tf_op jit(solution)/shard_map/ppermute | solution.py:89
  214.1 5.0 %copy-start.2 = (bf16[256,2048]{0,1:T(8,128)(2,1)S(1)}, bf16[256,2048]{0,1:T(8,128)(2,1)}, u32[]{:S(2)}) copy-start(bf16[256,2048]{0,1:T(8,128)(2,1)} %copy.33) | copy-start | bytes 3145732
  214.1 21.5 %collective-permute-start.11 = (bf16[256,2048]{1,0:T(8,128)(2,1)}, bf16[256,2048]{1,0:T(8,128)(2,1)}, u32[]{:S(2)}, u32[]{:S(2)}) collective-permute-start(bf16[256,2048]{1,0:T(8,128)(2,1)} %get-tuple-element.10), channel_id=1, source_target_pairs={{0,4},{4,0},{8,12},{12,8},{1,5},{5,1},{9,13},{13,9},{2,6},{6,2},{1... | collective-permute-start | bytes 3145736 | tf_op jit(solution)/shard_map/ppermute | solution.py:89
  260.6 3.3 %copy-start.1 = (bf16[2048,2048]{0,1:T(8,128)(2,1)}, bf16[2048,2048]{0,1:T(8,128)(2,1)S(1)}, u32[]{:S(2)}) copy-start(bf16[2048,2048]{0,1:T(8,128)(2,1)S(1)} %fusion.1) | copy-start | bytes 25165828
Sparse Core Ops, SparseCore 0:
  271.4 45.3 reduce-scatter.1

commit v2 on v1

--- a/solution.py
+++ b/solution.py
@@ -1,6 +1,8 @@
 import jax
 import jax.numpy as jnp
 from jax import lax
+from jax.experimental import pallas as pl
+from jax.experimental.pallas import tpu as pltpu
 from jax.sharding import PartitionSpec as P
 
 
@@ -50,27 +52,127 @@
 
 SIBLING = [(0, 1), (1, 0), (2, 3), (3, 2)]
 ACROSS = [(0, 2), (2, 0), (1, 3), (3, 1)]
-CHUNKS = 4
+CHUNKS = 8
+VMEM = 56 * 1024 * 1024
+
+
+def split_kernel(x_ref, first_ref, second_ref):
+    block, width = first_ref.shape
+    pairs = x_ref[...].reshape(2 * block, width)
+    row = lax.broadcasted_iota(jnp.int32, (2 * block, 2 * block), 0)
+    col = lax.broadcasted_iota(jnp.int32, (2 * block, 2 * block), 1)
+    source = jnp.where(row < block, 2 * row, 2 * (row - block) + 1)
+    order = (col == source).astype(jnp.bfloat16)
+    both = jnp.dot(order, pairs, preferred_element_type=jnp.float32).astype(jnp.bfloat16)
+    first_ref[...] = both[:block]
+    second_ref[...] = both[block:]
+
+
+def split_orbitals(three_center):
+    naux, _, _, nvirt = three_center.shape
+    block = 128
+    return pl.pallas_call(
+        split_kernel,
+        grid=(naux // block,),
+        in_specs=[pl.BlockSpec((block, 1, 2, nvirt), lambda i: (i, 0, 0, 0))],
+        out_specs=[pl.BlockSpec((block, nvirt), lambda i: (i, 0))] * 2,
+        out_shape=[jax.ShapeDtypeStruct((naux, nvirt), jnp.bfloat16)] * 2,
+        compiler_params=pltpu.CompilerParams(vmem_limit_bytes=VMEM),
+    )(three_center)
+
+
+def tilde_kernel(me_ref, own_ref, rows_ref, cols_ref, keep_ref, tilde_ref, density_ref):
+    slab, nvirt = rows_ref.shape
+    for j in range(nvirt // slab):
+        at = slice(j * slab, (j + 1) * slab)
+        mirrored = cols_ref[at, :].T.astype(jnp.float32)
+        value = 2.0 * rows_ref[:, at].astype(jnp.float32) - mirrored
+        tilde_ref[:, at] = (value * keep_ref[:, at]).astype(jnp.bfloat16)
+    density_ref[...] = lax.dot_general(
+        own_ref[...],
+        tilde_ref[...],
+        (((1,), (1,)), ((), ())),
+        preferred_element_type=jnp.float32,
+    ).astype(jnp.bfloat16)
+
+
+def tilde_density(me, amplitude, keep_row):
+    nvirt = amplitude.shape[0]
+    slab = nvirt // 4
+    return pl.pallas_call(
+        tilde_kernel,
+        grid_spec=pltpu.PrefetchScalarGridSpec(
+            num_scalar_prefetch=1,
+            grid=(4,),
+            in_specs=[
+                pl.BlockSpec((slab, nvirt), lambda i, s: (s[0], 0)),
+                pl.BlockSpec((slab, nvirt), lambda i, s: (i, 0)),
+                pl.BlockSpec((nvirt, slab), lambda i, s: (0, i)),
+                pl.BlockSpec((1, nvirt), lambda i, s: (0, 0)),
+            ],
+            out_specs=[
+                pl.BlockSpec((slab, nvirt), lambda i, s: (i, 0)),
+                pl.BlockSpec((slab, slab), lambda i, s: (0, i)),
+            ],
+        ),
+        out_shape=[
+            jax.ShapeDtypeStruct((nvirt, nvirt), jnp.bfloat16),
+            jax.ShapeDtypeStruct((slab, nvirt), jnp.bfloat16),
+        ],
+        compiler_params=pltpu.CompilerParams(vmem_limit_bytes=VMEM),
+    )(me.reshape(1), amplitude, amplitude, amplitude, keep_row)
+
+
+def gamma_kernel(second_ref, tilde_ref, gamma_ref):
+    gamma_ref[...] = lax.dot_general(
+        second_ref[...],
+        tilde_ref[...],
+        (((1,), (1,)), ((), ())),
+        preferred_element_type=jnp.float32,
+    ).astype(jnp.bfloat16)
+
+
+def gamma_of(second, tilde):
+    naux, nvirt = second.shape
+    block = 256
+    return pl.pallas_call(
+        gamma_kernel,
+        grid=(naux // block,),
+        in_specs=[
+            pl.BlockSpec((block, nvirt), lambda i: (i, 0)),
+            pl.BlockSpec((nvirt, nvirt), lambda i: (0, 0)),
+        ],
+        out_specs=pl.BlockSpec((block, nvirt), lambda i: (i, 0)),
+        out_shape=jax.ShapeDtypeStruct((naux, nvirt), jnp.bfloat16),
+        compiler_params=pltpu.CompilerParams(vmem_limit_bytes=VMEM),
+        cost_estimate=pl.CostEstimate(
+            flops=2 * naux * nvirt * nvirt,
+            bytes_accessed=4 * naux * nvirt + 2 * nvirt * nvirt,
+            transcendentals=0,
+        ),
+    )(second, tilde)
 
 
 def body(three_center, tile_mask, pair_orbitals, occ_energy, vir_energy):
-    nvirt = three_center.shape[3]
-    if lax.axis_size("aux") != 4 or three_center.shape[1] != 1 or nvirt % (CHUNKS * 512):
+    naux, npair, _, nvirt = three_center.shape
+    if lax.axis_size("aux") != 4 or npair != 1 or nvirt % (CHUNKS * 256) or naux % 256:
         return general_body(three_center, tile_mask, pair_orbitals, occ_energy, vir_energy)
-    slab = nvirt // 4
     width = nvirt // tile_mask.shape[2]
     keep = jnp.repeat(tile_mask[0], width, axis=1).astype(jnp.float32)
-    first = three_center[:, 0, 0, :]
-    second = three_center[:, 0, 1, :]
+    first, second = split_orbitals(three_center)
     shift = pick_shift(pair_orbitals, occ_energy)[0]
     me = lax.axis_index("aux")
     core = lax.rem(me, 2)
     rows = nvirt // CHUNKS
     half = rows // 2
-    amplitude = jnp.zeros((nvirt, nvirt), jnp.bfloat16)
+    source = first
+    chips = []
+    fars = []
     for k in range(CHUNKS):
+        if k >= 2:
+            source, chips[k - 2] = lax.optimization_barrier((source, chips[k - 2]))
         part = lax.dot_general(
-            first[:, k * rows : (k + 1) * rows],
+            source[:, k * rows : (k + 1) * rows],
             second,
             (((0,), (0,)), ((), ())),
             preferred_element_type=jnp.float32,
@@ -78,9 +180,11 @@
         mine = lax.dynamic_slice_in_dim(part, core * half, half, 0)
         other = lax.dynamic_slice_in_dim(part, (1 - core) * half, half, 0)
         got = lax.ppermute(other, "aux", SIBLING)
-        chip = (mine.astype(jnp.float32) + got.astype(jnp.float32)).astype(jnp.bfloat16)
-        far = lax.ppermute(chip, "aux", ACROSS)
-        total = chip.astype(jnp.float32) + far.astype(jnp.float32)
+        chips.append((mine.astype(jnp.float32) + got.astype(jnp.float32)).astype(jnp.bfloat16))
+    amplitude = jnp.zeros((nvirt, nvirt), jnp.bfloat16)
+    for k in range(CHUNKS):
+        far = lax.ppermute(chips[k], "aux", ACROSS)
+        total = chips[k].astype(jnp.float32) + far.astype(jnp.float32)
         start = k * rows + core * half
         vir_rows = lax.dynamic_slice_in_dim(vir_energy, start, half, 0)
         keep_rows = lax.dynamic_slice_in_dim(keep[0], start, half, 0)
@@ -91,18 +195,11 @@
         amplitude = lax.dynamic_update_slice_in_dim(
             amplitude, amp_other, k * rows + (1 - core) * half, 0
         )
-    wide = amplitude.astype(jnp.float32)
-    tilde = ((2.0 * wide - wide.T) * keep[1][None, :]).astype(jnp.bfloat16)
-    own = lax.dynamic_slice_in_dim(amplitude, me * slab, slab, 0)
-    density_part = lax.dot_general(
-        own, tilde, (((1,), (1,)), ((), ())), preferred_element_type=jnp.float32
-    )
+    tilde, density_part = tilde_density(me, amplitude, keep[1:2])
     vir_density = lax.psum_scatter(
-        density_part.astype(jnp.bfloat16), "occ", scatter_dimension=1, tiled=True
+        density_part, "occ", scatter_dimension=1, tiled=True
     ).astype(jnp.float32)
-    gamma = lax.dot_general(
-        second, tilde, (((1,), (1,)), ((), ())), preferred_element_type=jnp.float32
-    ).astype(jnp.bfloat16)
+    gamma = gamma_of(second, tilde)
     return (gamma[:, None, :], vir_density)
 
 

time: 327 us -> 248 us (0.76)
  local copies, waits for them, and re-layouts: 136 us -> 17.3 us
  Pallas kernels: 0 us -> 66.9 us
  matrix products: 59.1 us -> 35.3 us
  starting transfers between devices: 7.42 us -> 14.7 us
  other arithmetic: 25.7 us -> 18.8 us
  waiting for transfers between devices: 82.2 us -> 78.2 us
    pallas_call x0 -> x3, Pallas kernels: none -> 66.9 us  [the longest x1 28.5 us: gamma_of(): pl.pallas_call(gamma_kernel, grid=(naux // block,), in_specs=[pl.BlockSpe...]
    slice x1, local copies, waits for them, and re-layouts: 40.5 us -> 0.68 us  [body(): keep[1][None, :]]
    squeeze x1 -> x0, local copies, waits for them, and re-layouts: 27.2 us -> none  [body(): second = three_center[:, 0, 1, :]]
    dot_general x6 -> x8, matrix products: 59.1 us -> 35.3 us  [body(): lax.dot_general(source[:, k * rows:(k + 1) * rows], second, (((0,), (0,))...]
    convert_element_type x5 -> x0, local copies, waits for them, and re-layouts: 19.8 us -> none  [the longest x1 13.1 us: body(): wide = amplitude.astype(jnp.float32)]
    unnamed x23 -> x44, local copies, waits for them, and re-layouts: 20 us -> 0.88 us
    ppermute x4 -> x8, waiting for transfers between devices: 79.7 us -> 60.8 us  [body(): far = lax.ppermute(chips[k], 'aux', ACROSS)]
    convert_element_type x3 -> x1, other arithmetic: 17.2 us -> 2.14 us  [body(): vir_density = lax.psum_scatter(density_part, 'occ', scatter_dimension=1,...]
  transfers between devices with their start and end apart: 13 -> 25, of which waited for: 5 -> 9; matrix products, arithmetic and copies ran while one was open for 31% -> 23% of each run, Pallas kernels for 0% -> 12%
where the time goes in v2:
time: 248 us; the launch traced here: 247 us
  waiting for transfers between devices  78.2 us (32%)
  Pallas kernels  66.9 us (27%)
  matrix products  35.3 us (14%)
  other arithmetic  18.8 us (8%)
  local copies, waits for them, and re-layouts  17.3 us (7%)
  between operations  15.7 us (6%)
  starting transfers between devices  14.7 us (6%)
    ppermute x8, waiting for transfers between devices, body(): far = lax.ppermute(chips[k], 'aux', ACROSS)  60.8 us
    dot_general x8, matrix products, body(): lax.dot_general(source[:, k * rows:(k + 1) * rows], second, (((0,), (0,))...  35.3 us
    pallas_call x1, Pallas kernels, gamma_of(): pl.pallas_call(gamma_kernel, grid=(naux // block,), in_specs=[pl.BlockSpe...  28.5 us
    pallas_call x1, Pallas kernels, split_orbitals(): pl.pallas_call(split_kernel, grid=(naux // block,), in_specs=[pl.BlockSpe...  24.9 us
    reduce_scatter x1, waiting for transfers between devices, body(): lax.psum_scatter(density_part, 'occ', scatter_dimension=1, tiled=True)  16.1 us
    pallas_call x1, Pallas kernels, tilde_density(): pl.pallas_call(tilde_kernel, grid_spec=pltpu.PrefetchScalarGridSpec(num_s...  13.5 us
    dynamic_update_slice x8, other arithmetic, body(): amplitude = lax.dynamic_update_slice_in_dim(amplitude, amp, start, 0)  12.9 us
    ppermute x8, starting transfers between devices, body(): far = lax.ppermute(chips[k], 'aux', ACROSS)  11 us
  transfers between devices with their start and end apart: 25, of which 9 were waited for; matrix products, arithmetic and copies ran while one was open for 23% of the time, Pallas kernels for 12%

profile of v2, /device:TPU:0, one launch (start us, length us, event | category | flops | bytes accessed | tf_op | source)
XLA Modules:
  0.0 246.8 jit_solution(7834079838728513023)
XLA Ops:
  7.2 24.9 %shard_map.71 = (bf16[2560,2048]{1,0:T(8,128)(2,1)}, bf16[2560,2048]{1,0:T(8,128)(2,1)}) custom-call(bf16[2560,1,2,2048]{3,2,1,0:T(2,128)(2,1)} %x_ref.1), custom_call_target="tpu_custom_call" | custom-call | tf_op jit(solution)/shard_map/pallas_call | solution.py:74
  32.1 7.4 %convolution_convert_fusion.6 = bf16[256,2048]{1,0:T(8,128)(2,1)S(1)} fusion(bf16[2560,2048]{1,0:T(8,128)(2,1)} %get-tuple-element.18.second_ref, bf16[2560,2048]{1,0:T(8,128)(2,1)} %get-tuple-element.31), kind=kOutput, calls=%fused_computation.6 | convolution fusion | flops 2684878848 | bytes 12845056 | tf_op jit(solution)/shard_map/dot_general | solution.py:174
  40.9 4.2 %convolution_convert_fusion.7 = bf16[256,2048]{1,0:T(8,128)(2,1)S(1)} fusion(bf16[2560,2048]{1,0:T(8,128)(2,1)S(1)} %copy-done, bf16[2560,2048]{1,0:T(8,128)(2,1)} %get-tuple-element.31), kind=kOutput, calls=%fused_computation.7 | convolution fusion | flops 2684878848 | bytes 12845056 | tf_op jit(solution)/shard_map/dot_general | solution.py:174
  50.0 7.5 %convolution_convert_fusion.5 = bf16[256,2048]{1,0:T(8,128)(2,1)S(1)} fusion(bf16[2560,2048]{1,0:T(8,128)(2,1)} %get-tuple-element.18.second_ref, bf16[2560,2048]{1,0:T(8,128)(2,1)} %get-tuple-element.31), kind=kOutput, calls=%fused_computation.5 | convolution fusion | flops 2684878848 | bytes 12845056 | tf_op jit(solution)/shard_map/dot_general | solution.py:174
  59.1 4.4 %convolution_convert_fusion.4 = bf16[256,2048]{1,0:T(8,128)(2,1)S(1)} fusion(bf16[2560,2048]{1,0:T(8,128)(2,1)S(1)} %bitcast.34, bf16[2560,2048]{1,0:T(8,128)(2,1)} %get-tuple-element.31), kind=kOutput, calls=%fused_computation.4 | convolution fusion | flops 2684878848 | bytes 12845056 | tf_op jit(solution)/shard_map/dot_general | solution.py:174
  63.5 2.6 %collective-permute-start.1 = (bf16[128,2048]{1,0:T(8,128)(2,1)S(1)}, bf16[128,2048]{1,0:T(8,128)(2,1)S(1)}, u32[]{:S(2)}, u32[]{:S(2)}) collective-permute-start(bf16[128,2048]{1,0:T(8,128)(2,1)S(1)} %add_convert_fusion.7), channel_id=1, source_target_pairs={{0,8},{8,0},{4,12},{12,4},{1,9},{9,1},{5,13},{13,5},{2,10},{10,2},... | collective-permute-start | bytes 1572872 | tf_op jit(solution)/shard_map/ppermute | solution.py:186
  67.6 11.3 %collective-permute-done.1 = bf16[128,2048]{1,0:T(8,128)(2,1)S(1)} collective-permute-done((bf16[128,2048]{1,0:T(8,128)(2,1)S(1)}, bf16[128,2048]{1,0:T(8,128)(2,1)S(1)}, u32[]{:S(2)}, u32[]{:S(2)}) %collective-permute-start.1) | collective-permute-done | bytes 524320 | tf_op jit(solution)/shard_map/ppermute | solution.py:186
  79.7 4.5 %broadcast_in_dim.20 = bf16[2048,2048]{1,0:T(8,128)(2,1)} broadcast(bf16[]{:T(256)} %constant.43.clone.1), dimensions={} | broadcast | bytes 8388610 | tf_op jit(solution)/shard_map/broadcast_in_dim | solution.py:184
  84.1 2.5 constant_dynamic-update-slice_fusion.15
  86.6 3.1 %convolution_convert_fusion.3 = bf16[256,2048]{1,0:T(8,128)(2,1)S(1)} fusion(bf16[2560,2048]{1,0:T(8,128)(2,1)S(1)} %bitcast.34, bf16[2560,2048]{1,0:T(8,128)(2,1)S(1)} %bitcast.36), kind=kOutput, calls=%fused_computation.3 | convolution fusion | flops 2684878848 | bytes 12845056 | tf_op jit(solution)/shard_map/dot_general | solution.py:174
  91.0 2.0 collective-permute-start.7
  93.8 2.5 %constant_dynamic-update-slice_fusion.13 = (bf16[2048,2048]{1,0:T(8,128)(2,1)}, bf16[128,2048]{1,0:T(8,128)(2,1)S(1)}) fusion(bf16[2048,2048]{1,0:T(8,128)(2,1)} %constant_dynamic-update-slice_fusion.14, s32[]{:T(128)S(6)} %select_n.101, f32[2048]{0:T(1024)S(1)} %mul.77, f32[128]{0:T(128)S(1)} %copy-done.12, f32[2048]{0:T(1024)S(1)} %copy-done.2, ...), kind=kLoop, calls=%fused_computation.57 | loop fusion | flops 2097152 | bytes 2114564 | tf_op jit(solution)/shard_map/dynamic_update_slice | solution.py:194
  96.6 2.9 %convolution_convert_fusion.2 = bf16[256,2048]{1,0:T(8,128)(2,1)S(1)} fusion(bf16[2560,2048]{1,0:T(8,128)(2,1)S(1)} %bitcast.34, bf16[2560,2048]{1,0:T(8,128)(2,1)S(1)} %bitcast.36), kind=kOutput, calls=%fused_computation.2 | convolution fusion | flops 2684878848 | bytes 12845056 | tf_op jit(solution)/shard_map/dot_general | solution.py:174
  100.8 4.7 %collective-permute-done.7 = bf16[128,2048]{1,0:T(8,128)(2,1)S(1)} collective-permute-done((bf16[128,2048]{1,0:T(8,128)(2,1)S(1)}, bf16[128,2048]{1,0:T(8,128)(2,1)S(1)}, u32[]{:S(2)}, u32[]{:S(2)}) %collective-permute-start.7) | collective-permute-done | bytes 524320 | tf_op jit(solution)/shard_map/ppermute | solution.py:186
  105.5 1.3 constant_dynamic-update-slice_fusion.11
  107.5 1.7 collective-permute-start.10
  110.6 11.7 %collective-permute-done.10 = bf16[128,2048]{1,0:T(8,128)(2,1)S(1)} collective-permute-done((bf16[128,2048]{1,0:T(8,128)(2,1)S(1)}, bf16[128,2048]{1,0:T(8,128)(2,1)S(1)}, u32[]{:S(2)}, u32[]{:S(2)}) %collective-permute-start.10) | collective-permute-done | bytes 524320 | tf_op jit(solution)/shard_map/ppermute | solution.py:186
  123.5 2.9 %convolution_convert_fusion.1 = bf16[256,2048]{1,0:T(8,128)(2,1)S(1)} fusion(bf16[2560,2048]{1,0:T(8,128)(2,1)S(1)} %bitcast.34, bf16[2560,2048]{1,0:T(8,128)(2,1)S(1)} %bitcast.36), kind=kOutput, calls=%fused_computation.1 | convolution fusion | flops 2684878848 | bytes 12845056 | tf_op jit(solution)/shard_map/dot_general | solution.py:174
  127.9 4.7 %collective-permute-done.13 = bf16[128,2048]{1,0:T(8,128)(2,1)S(1)} collective-permute-done((bf16[128,2048]{1,0:T(8,128)(2,1)S(1)}, bf16[128,2048]{1,0:T(8,128)(2,1)S(1)}, u32[]{:S(2)}, u32[]{:S(2)}) %collective-permute-start.13) | collective-permute-done | bytes 524320 | tf_op jit(solution)/shard_map/ppermute | solution.py:186
  134.0 1.8 collective-permute-start.16
  137.2 11.6 %collective-permute-done.16 = bf16[128,2048]{1,0:T(8,128)(2,1)S(1)} collective-permute-done((bf16[128,2048]{1,0:T(8,128)(2,1)S(1)}, bf16[128,2048]{1,0:T(8,128)(2,1)S(1)}, u32[]{:S(2)}, u32[]{:S(2)}) %collective-permute-start.16) | collective-permute-done | bytes 524320 | tf_op jit(solution)/shard_map/ppermute | solution.py:186
  148.8 1.3 constant_dynamic-update-slice_fusion.5
  150.1 2.9 %convolution_convert_fusion = bf16[256,2048]{1,0:T(8,128)(2,1)S(1)} fusion(bf16[2560,2048]{1,0:T(8,128)(2,1)S(1)} %bitcast.34, bf16[2560,2048]{1,0:T(8,128)(2,1)S(1)} %bitcast.36), kind=kOutput, calls=%fused_computation | convolution fusion | flops 2684878848 | bytes 12845056 | tf_op jit(solution)/shard_map/dot_general | solution.py:174
  154.6 5.1 %collective-permute-done.19 = bf16[128,2048]{1,0:T(8,128)(2,1)S(1)} collective-permute-done((bf16[128,2048]{1,0:T(8,128)(2,1)S(1)}, bf16[128,2048]{1,0:T(8,128)(2,1)S(1)}, u32[]{:S(2)}, u32[]{:S(2)}) %collective-permute-start.19) | collective-permute-done | bytes 524320 | tf_op jit(solution)/shard_map/ppermute | solution.py:186
  159.6 1.5 constant_dynamic-update-slice_fusion.3
  161.3 1.8 collective-permute-start.22
  163.9 11.8 %collective-permute-done.22 = bf16[128,2048]{1,0:T(8,128)(2,1)S(1)} collective-permute-done((bf16[128,2048]{1,0:T(8,128)(2,1)S(1)}, bf16[128,2048]{1,0:T(8,128)(2,1)S(1)}, u32[]{:S(2)}, u32[]{:S(2)}) %collective-permute-start.22) | collective-permute-done | bytes 524320 | tf_op jit(solution)/shard_map/ppermute | solution.py:186
  175.7 1.3 constant_dynamic-update-slice_fusion.1
  179.7 13.5 %shard_map.72 = (bf16[2048,2048]{1,0:T(8,128)(2,1)}, bf16[512,2048]{1,0:T(8,128)(2,1)}) custom-call(s32[1]{0:T(128)} %bitcast.me_ref, bf16[2048,2048]{1,0:T(8,128)(2,1)} %constant_dynamic-update-slice_fusion.own_ref.rows_ref.cols_ref, bf16[2048,2048]{1,0:T(8,128)(2,1)} %constant_dynamic-update-slice_fusion.own_ref.rows_ref.cols_ref, ...), custom_call_target="tpu_custom_call" | custom-call | tf_op jit(solution)/shard_map/pallas_call | solution.py:102
  193.3 28.5 %shard_map.73 = bf16[2560,2048]{1,0:T(8,128)(2,1)} custom-call(bf16[2560,2048]{1,0:T(8,128)(2,1)} %get-tuple-element.18.second_ref, bf16[2048,2048]{1,0:T(8,128)(2,1)} %get-tuple-element.32.tilde_ref), custom_call_target="tpu_custom_call" | custom-call | flops 21474836480 | bytes 29360128 | tf_op jit(solution)/shard_map/pallas_call | solution.py:138
  221.7 16.1 %reduce-scatter.2.cloned.1.call-done = bf16[512,512]{1,0:T(8,128)(2,1)} async-done(((bf16[512,2048]{1,0:T(8,128)(2,1)}), bf16[512,512]{1,0:T(8,128)(2,1)}) %reduce-scatter.2.cloned.1.call-update) | async-done | bytes 524304 | tf_op jit(solution)/shard_map/reduce_scatter | solution.py:199
  237.8 2.1 convert_element_type.234
  (121 shorter events, 25.1 us)
Async XLA Ops:
  7.2 230.6 %reduce-scatter.2.cloned.1.call-start = ((), (), s32[]{:S(2)}) async-start(), calls=%async_computation.1 | async-start | bytes 2621440 | tf_op jit(solution)/shard_map/reduce_scatter | solution.py:199
  40.4 17.1 %collective-permute-start.3 = (bf16[128,2048]{1,0:T(8,128)(2,1)}, bf16[128,2048]{1,0:T(8,128)(2,1)S(1)}, u32[]{:S(2)}, u32[]{:S(2)}) collective-permute-start(bf16[128,2048]{1,0:T(8,128)(2,1)} %constant_dynamic-slice_fusion.13), channel_id=1, source_target_pairs={{0,4},{4,0},{8,12},{12,8},{1,5},{5,1},{9,13},{13,9},{2,6},{6,2},{1... | collective-permute-start | bytes 1572872 | tf_op jit(solution)/shard_map/ppermute | solution.py:182
  46.0 3.9 %collective-permute-start = (bf16[128,2048]{1,0:T(8,128)(2,1)}, bf16[128,2048]{1,0:T(8,128)(2,1)S(1)}, u32[]{:S(2)}, u32[]{:S(2)}) collective-permute-start(bf16[128,2048]{1,0:T(8,128)(2,1)} %constant_dynamic-slice_fusion.15), channel_id=1, source_target_pairs={{0,4},{4,0},{8,12},{12,8},{1,5},{5,1},{9,13},{13,9},{2,6},{6,2},{1... | collective-permute-start | bytes 1572872 | tf_op jit(solution)/shard_map/ppermute | solution.py:182
  50.0 13.5 %copy-start.1 = (bf16[128,2048]{1,0:T(8,128)(2,1)}, bf16[128,2048]{1,0:T(8,128)(2,1)S(1)}, u32[]{:S(2)}) copy-start(bf16[128,2048]{1,0:T(8,128)(2,1)S(1)} %add_convert_fusion.7) | copy-start | bytes 1572868
  58.5 8.9 %collective-permute-start.6 = (bf16[128,2048]{1,0:T(8,128)(2,1)S(1)}, bf16[128,2048]{1,0:T(8,128)(2,1)S(1)}, u32[]{:S(2)}, u32[]{:S(2)}) collective-permute-start(bf16[128,2048]{1,0:T(8,128)(2,1)S(1)} %constant_dynamic-slice_fusion.11), channel_id=1, source_target_pairs={{0,4},{4,0},{8,12},{12,8},{1,5},{5,1},{9,13},{13,9},{2,6},{6,2},{1... | collective-permute-start | bytes 1572872 | tf_op jit(solution)/shard_map/ppermute | solution.py:182
  59.1 27.5 %slice-start.3 = ((s8[10485760]{0:T(1024)(128)(4,1)}), s8[4194304]{0:T(1024)(128)(4,1)S(1)}, s32[]{:S(2)}) async-start(s8[10485760]{0:T(1024)(128)(4,1)} %bitcast.35), calls=%async_computation.5 | async-start | bytes 8388608
  59.1 27.5 %slice-start.4 = ((s8[10485760]{0:T(1024)(128)(4,1)}), s8[4194304]{0:T(1024)(128)(4,1)S(1)}, s32[]{:S(2)}) async-start(s8[10485760]{0:T(1024)(128)(4,1)} %bitcast.35), calls=%async_computation.6 | async-start | bytes 8388608
  63.5 15.4 %collective-permute-start.1 = (bf16[128,2048]{1,0:T(8,128)(2,1)S(1)}, bf16[128,2048]{1,0:T(8,128)(2,1)S(1)}, u32[]{:S(2)}, u32[]{:S(2)}) collective-permute-start(bf16[128,2048]{1,0:T(8,128)(2,1)S(1)} %add_convert_fusion.7), channel_id=1, source_target_pairs={{0,8},{8,0},{4,12},{12,4},{1,9},{9,1},{5,13},{13,5},{2,10},{10,2},... | collective-permute-start | bytes 1572872 | tf_op jit(solution)/shard_map/ppermute | solution.py:186
  67.0 19.6 %slice-start.5 = ((s8[10485760]{0:T(1024)(128)(4,1)}), s8[2097152]{0:T(1024)(128)(4,1)S(1)}, s32[]{:S(2)}) async-start(s8[10485760]{0:T(1024)(128)(4,1)} %bitcast.35), calls=%async_computation.7 | async-start | bytes 4194304
  67.0 22.8 %collective-permute-start.9 = (bf16[128,2048]{1,0:T(8,128)(2,1)}, bf16[128,2048]{1,0:T(8,128)(2,1)}, u32[]{:S(2)}, u32[]{:S(2)}) collective-permute-start(bf16[128,2048]{1,0:T(8,128)(2,1)} %constant_dynamic-slice_fusion.9), channel_id=1, source_target_pairs={{0,4},{4,0},{8,12},{12,8},{1,5},{5,1},{9,13},{13,9},{2,6},{6,2},{1... | collective-permute-start | bytes 1572872 | tf_op jit(solution)/shard_map/ppermute | solution.py:182
  67.2 26.7 %collective-permute-start.4 = (bf16[128,2048]{1,0:T(8,128)(2,1)}, bf16[128,2048]{1,0:T(8,128)(2,1)}, u32[]{:S(2)}, u32[]{:S(2)}) collective-permute-start(bf16[128,2048]{1,0:T(8,128)(2,1)} %add_convert_fusion.6), channel_id=1, source_target_pairs={{0,8},{8,0},{4,12},{12,4},{1,9},{9,1},{5,13},{13,5},{2,10},{10,2},... | collective-permute-start | bytes 1572872 | tf_op jit(solution)/shard_map/ppermute | solution.py:186
  86.6 6.4 %collective-permute-start.2 = (bf16[128,2048]{1,0:T(8,128)(2,1)S(1)}, bf16[128,2048]{1,0:T(8,128)(2,1)S(1)}, u32[]{:S(2)}, u32[]{:S(2)}) collective-permute-start(bf16[128,2048]{1,0:T(8,128)(2,1)S(1)} %get-tuple-element.49), channel_id=1, source_target_pairs={{0,4},{4,0},{8,12},{12,8},{1,5},{5,1},{9,13},{13,9},{2,6},{6,2},{1... | collective-permute-start | bytes 1572872 | tf_op jit(solution)/shard_map/ppermute | solution.py:193
  91.0 14.6 %collective-permute-start.7 = (bf16[128,2048]{1,0:T(8,128)(2,1)S(1)}, bf16[128,2048]{1,0:T(8,128)(2,1)S(1)}, u32[]{:S(2)}, u32[]{:S(2)}) collective-permute-start(bf16[128,2048]{1,0:T(8,128)(2,1)S(1)} %add_convert_fusion.5), channel_id=1, source_target_pairs={{0,8},{8,0},{4,12},{12,4},{1,9},{9,1},{5,13},{13,5},{2,10},{10,2},... | collective-permute-start | bytes 1572872 | tf_op jit(solution)/shard_map/ppermute | solution.py:186
  96.3 25.9 %copy-start.8 = (f32[128]{0:T(128)S(1)}, f32[128]{0:T(128)}, u32[]{:S(2)}) copy-start(f32[128]{0:T(128)} %get-tuple-element.62) | copy-start | bytes 1540
  96.3 25.9 %copy-start.9 = (f32[128]{0:T(128)S(1)}, f32[128]{0:T(128)}, u32[]{:S(2)}) copy-start(f32[128]{0:T(128)} %get-tuple-element.53) | copy-start | bytes 1540
  96.3 3.6 %collective-permute-start.5 = (bf16[128,2048]{1,0:T(8,128)(2,1)S(1)}, bf16[128,2048]{1,0:T(8,128)(2,1)S(1)}, u32[]{:S(2)}, u32[]{:S(2)}) collective-permute-start(bf16[128,2048]{1,0:T(8,128)(2,1)S(1)} %get-tuple-element.47), channel_id=1, source_target_pairs={{0,4},{4,0},{8,12},{12,8},{1,5},{5,1},{9,13},{13,9},{2,6},{6,2},{1... | collective-permute-start | bytes 1572872 | tf_op jit(solution)/shard_map/ppermute | solution.py:193
  99.5 9.7 %collective-permute-start.12 = (bf16[128,2048]{1,0:T(8,128)(2,1)S(1)}, bf16[128,2048]{1,0:T(8,128)(2,1)S(1)}, u32[]{:S(2)}, u32[]{:S(2)}) collective-permute-start(bf16[128,2048]{1,0:T(8,128)(2,1)S(1)} %constant_dynamic-slice_fusion.7), channel_id=1, source_target_pairs={{0,4},{4,0},{8,12},{12,8},{1,5},{5,1},{9,13},{13,9},{2,6},{6,2},{1... | collective-permute-start | bytes 1572872 | tf_op jit(solution)/shard_map/ppermute | solution.py:182
  106.8 2.9 %collective-permute-start.8 = (bf16[128,2048]{1,0:T(8,128)(2,1)S(1)}, bf16[128,2048]{1,0:T(8,128)(2,1)S(1)}, u32[]{:S(2)}, u32[]{:S(2)}) collective-permute-start(bf16[128,2048]{1,0:T(8,128)(2,1)S(1)} %get-tuple-element.45), channel_id=1, source_target_pairs={{0,4},{4,0},{8,12},{12,8},{1,5},{5,1},{9,13},{13,9},{2,6},{6,2},{1... | collective-permute-start | bytes 1572872 | tf_op jit(solution)/shard_map/ppermute | solution.py:193
  106.9 27.0 %collective-permute-start.15 = (bf16[128,2048]{1,0:T(8,128)(2,1)S(1)}, bf16[128,2048]{1,0:T(8,128)(2,1)S(1)}, u32[]{:S(2)}, u32[]{:S(2)}) collective-permute-start(bf16[128,2048]{1,0:T(8,128)(2,1)S(1)} %constant_dynamic-slice_fusion.5), channel_id=1, source_target_pairs={{0,4},{4,0},{8,12},{12,8},{1,5},{5,1},{9,13},{13,9},{2,6},{6,2},{1... | collective-permute-start | bytes 1572872 | tf_op jit(solution)/shard_map/ppermute | solution.py:182
  107.5 14.8 %collective-permute-start.10 = (bf16[128,2048]{1,0:T(8,128)(2,1)S(1)}, bf16[128,2048]{1,0:T(8,128)(2,1)S(1)}, u32[]{:S(2)}, u32[]{:S(2)}) collective-permute-start(bf16[128,2048]{1,0:T(8,128)(2,1)S(1)} %add_convert_fusion.4), channel_id=1, source_target_pairs={{0,8},{8,0},{4,12},{12,4},{1,9},{9,1},{5,13},{13,5},{2,10},{10,2},... | collective-permute-start | bytes 1572872 | tf_op jit(solution)/shard_map/ppermute | solution.py:186
  109.3 23.3 %collective-permute-start.13 = (bf16[128,2048]{1,0:T(8,128)(2,1)S(1)}, bf16[128,2048]{1,0:T(8,128)(2,1)S(1)}, u32[]{:S(2)}, u32[]{:S(2)}) collective-permute-start(bf16[128,2048]{1,0:T(8,128)(2,1)S(1)} %add_convert_fusion.3), channel_id=1, source_target_pairs={{0,8},{8,0},{4,12},{12,4},{1,9},{9,1},{5,13},{13,5},{2,10},{10,2},... | collective-permute-start | bytes 1572872 | tf_op jit(solution)/shard_map/ppermute | solution.py:186
  123.5 3.5 %collective-permute-start.11 = (bf16[128,2048]{1,0:T(8,128)(2,1)S(1)}, bf16[128,2048]{1,0:T(8,128)(2,1)S(1)}, u32[]{:S(2)}, u32[]{:S(2)}) collective-permute-start(bf16[128,2048]{1,0:T(8,128)(2,1)S(1)} %get-tuple-element.43), channel_id=1, source_target_pairs={{0,4},{4,0},{8,12},{12,8},{1,5},{5,1},{9,13},{13,9},{2,6},{6,2},{1... | collective-permute-start | bytes 1572872 | tf_op jit(solution)/shard_map/ppermute | solution.py:193
  126.4 22.4 %copy-start.5 = (f32[128]{0:T(128)S(1)}, f32[128]{0:T(128)}, u32[]{:S(2)}) copy-start(f32[128]{0:T(128)} %get-tuple-element.51) | copy-start | bytes 1540
  126.5 9.3 %collective-permute-start.18 = (bf16[128,2048]{1,0:T(8,128)(2,1)S(1)}, bf16[128,2048]{1,0:T(8,128)(2,1)S(1)}, u32[]{:S(2)}, u32[]{:S(2)}) collective-permute-start(bf16[128,2048]{1,0:T(8,128)(2,1)S(1)} %constant_dynamic-slice_fusion.3), channel_id=1, source_target_pairs={{0,4},{4,0},{8,12},{12,8},{1,5},{5,1},{9,13},{13,9},{2,6},{6,2},{1... | collective-permute-start | bytes 1572872 | tf_op jit(solution)/shard_map/ppermute | solution.py:182
  133.9 2.4 collective-permute-start.14
  134.0 14.8 %collective-permute-start.16 = (bf16[128,2048]{1,0:T(8,128)(2,1)S(1)}, bf16[128,2048]{1,0:T(8,128)(2,1)S(1)}, u32[]{:S(2)}, u32[]{:S(2)}) collective-permute-start(bf16[128,2048]{1,0:T(8,128)(2,1)S(1)} %add_convert_fusion.2), channel_id=1, source_target_pairs={{0,8},{8,0},{4,12},{12,4},{1,9},{9,1},{5,13},{13,5},{2,10},{10,2},... | collective-permute-start | bytes 1572872 | tf_op jit(solution)/shard_map/ppermute | solution.py:186
  136.0 23.7 %collective-permute-start.19 = (bf16[128,2048]{1,0:T(8,128)(2,1)S(1)}, bf16[128,2048]{1,0:T(8,128)(2,1)S(1)}, u32[]{:S(2)}, u32[]{:S(2)}) collective-permute-start(bf16[128,2048]{1,0:T(8,128)(2,1)S(1)} %add_convert_fusion.1), channel_id=1, source_target_pairs={{0,8},{8,0},{4,12},{12,4},{1,9},{9,1},{5,13},{13,5},{2,10},{10,2},... | collective-permute-start | bytes 1572872 | tf_op jit(solution)/shard_map/ppermute | solution.py:186
  150.1 3.5 %collective-permute-start.17 = (bf16[128,2048]{1,0:T(8,128)(2,1)S(1)}, bf16[128,2048]{1,0:T(8,128)(2,1)S(1)}, u32[]{:S(2)}, u32[]{:S(2)}) collective-permute-start(bf16[128,2048]{1,0:T(8,128)(2,1)S(1)} %get-tuple-element.39), channel_id=1, source_target_pairs={{0,4},{4,0},{8,12},{12,8},{1,5},{5,1},{9,13},{13,9},{2,6},{6,2},{1... | collective-permute-start | bytes 1572872 | tf_op jit(solution)/shard_map/ppermute | solution.py:193
  153.1 8.1 %collective-permute-start.21 = (bf16[128,2048]{1,0:T(8,128)(2,1)S(1)}, bf16[128,2048]{1,0:T(8,128)(2,1)S(1)}, u32[]{:S(2)}, u32[]{:S(2)}) collective-permute-start(bf16[128,2048]{1,0:T(8,128)(2,1)S(1)} %constant_dynamic-slice_fusion.1), channel_id=1, source_target_pairs={{0,4},{4,0},{8,12},{12,8},{1,5},{5,1},{9,13},{13,9},{2,6},{6,2},{1... | collective-permute-start | bytes 1572872 | tf_op jit(solution)/shard_map/ppermute | solution.py:182
  161.1 1.9 collective-permute-start.20
  161.3 14.4 %collective-permute-start.22 = (bf16[128,2048]{1,0:T(8,128)(2,1)S(1)}, bf16[128,2048]{1,0:T(8,128)(2,1)S(1)}, u32[]{:S(2)}, u32[]{:S(2)}) collective-permute-start(bf16[128,2048]{1,0:T(8,128)(2,1)S(1)} %add_convert_fusion), channel_id=1, source_target_pairs={{0,8},{8,0},{4,12},{12,4},{1,9},{9,1},{5,13},{13,5},{2,10},{10,2},... | collective-permute-start | bytes 1572872 | tf_op jit(solution)/shard_map/ppermute | solution.py:186
  177.0 1.9 collective-permute-start.23
  (15 other events, 114.3 us)
Sparse Core Ops, SparseCore 0:
  193.4 44.3 reduce-scatter.1

commit v3 on v2

--- a/solution.py
+++ b/solution.py
@@ -52,7 +52,6 @@
 
 SIBLING = [(0, 1), (1, 0), (2, 3), (3, 2)]
 ACROSS = [(0, 2), (2, 0), (1, 3), (3, 1)]
-CHUNKS = 8
 VMEM = 56 * 1024 * 1024
 
 
@@ -155,7 +154,7 @@
 
 def body(three_center, tile_mask, pair_orbitals, occ_energy, vir_energy):
     naux, npair, _, nvirt = three_center.shape
-    if lax.axis_size("aux") != 4 or npair != 1 or nvirt % (CHUNKS * 256) or naux % 256:
+    if lax.axis_size("aux") != 4 or npair != 1 or nvirt % 2048 or naux % 256:
         return general_body(three_center, tile_mask, pair_orbitals, occ_energy, vir_energy)
     width = nvirt // tile_mask.shape[2]
     keep = jnp.repeat(tile_mask[0], width, axis=1).astype(jnp.float32)
@@ -163,16 +162,16 @@
     shift = pick_shift(pair_orbitals, occ_energy)[0]
     me = lax.axis_index("aux")
     core = lax.rem(me, 2)
-    rows = nvirt // CHUNKS
-    half = rows // 2
+    unit = nvirt // 8
+    spans = [(k * unit, (k + 1) * unit) for k in range(8)]
     source = first
     chips = []
-    fars = []
-    for k in range(CHUNKS):
+    for k, (low, high) in enumerate(spans):
+        half = (high - low) // 2
         if k >= 2:
             source, chips[k - 2] = lax.optimization_barrier((source, chips[k - 2]))
         part = lax.dot_general(
-            source[:, k * rows : (k + 1) * rows],
+            source[:, low:high],
             second,
             (((0,), (0,)), ((), ())),
             preferred_element_type=jnp.float32,
@@ -181,20 +180,22 @@
         other = lax.dynamic_slice_in_dim(part, (1 - core) * half, half, 0)
         got = lax.ppermute(other, "aux", SIBLING)
         chips.append((mine.astype(jnp.float32) + got.astype(jnp.float32)).astype(jnp.bfloat16))
+    fars = [lax.ppermute(chip, "aux", ACROSS) for chip in chips]
+    held = lax.optimization_barrier(tuple(fars[:6] + chips[6:]))
+    fars[:6], chips[6:] = held[:6], held[6:]
     amplitude = jnp.zeros((nvirt, nvirt), jnp.bfloat16)
-    for k in range(CHUNKS):
-        far = lax.ppermute(chips[k], "aux", ACROSS)
-        total = chips[k].astype(jnp.float32) + far.astype(jnp.float32)
-        start = k * rows + core * half
+    for chip, far, (low, high) in zip(chips, fars, spans):
+        half = (high - low) // 2
+        start = low + core * half
+        away = low + (1 - core) * half
+        total = chip.astype(jnp.float32) + far.astype(jnp.float32)
         vir_rows = lax.dynamic_slice_in_dim(vir_energy, start, half, 0)
         keep_rows = lax.dynamic_slice_in_dim(keep[0], start, half, 0)
         denominator = shift - vir_rows[:, None] - vir_energy[None, :]
         amp = (total / denominator * keep_rows[:, None] * keep[1][None, :]).astype(jnp.bfloat16)
         amp_other = lax.ppermute(amp, "aux", SIBLING)
         amplitude = lax.dynamic_update_slice_in_dim(amplitude, amp, start, 0)
-        amplitude = lax.dynamic_update_slice_in_dim(
-            amplitude, amp_other, k * rows + (1 - core) * half, 0
-        )
+        amplitude = lax.dynamic_update_slice_in_dim(amplitude, amp_other, away, 0)
     tilde, density_part = tilde_density(me, amplitude, keep[1:2])
     vir_density = lax.psum_scatter(
         density_part, "occ", scatter_dimension=1, tiled=True

time: 248 us -> 278 us (1.12)
  waiting for transfers between devices: 78.2 us -> 105 us
  other arithmetic: 18.8 us -> 25.9 us
  starting transfers between devices: 14.7 us -> 10.8 us
    ppermute x8, waiting for transfers between devices: 60.8 us -> 74.9 us  [body(): fars = [lax.ppermute(chip, 'aux', ACROSS) for chip in chips]]
    ppermute x8, waiting for transfers between devices: 1.25 us -> 14.1 us  [body(): amp_other = lax.ppermute(amp, 'aux', SIBLING)]
    convert_element_type x8, other arithmetic: 2.87 us -> 7.17 us  [body(): (mine.astype(jnp.float32) + got.astype(jnp.float32)).astype(jnp.bfloat16)]
    dynamic_update_slice x8, other arithmetic: 12.9 us -> 16.2 us  [body(): amplitude = lax.dynamic_update_slice_in_dim(amplitude, amp, start, 0)]
    ppermute x8, starting transfers between devices: 11 us -> 7.8 us  [body(): fars = [lax.ppermute(chip, 'aux', ACROSS) for chip in chips]]
  transfers between devices with their start and end apart: 25 -> 25, of which waited for: 9 -> 16; matrix products, arithmetic and copies ran while one was open for 23% -> 15% of each run, Pallas kernels for 12% -> 10%
where the time goes in v3:
time: 278 us; the launch traced here: 277 us
  waiting for transfers between devices  105 us (38%)
  Pallas kernels  66.7 us (24%)
  matrix products  35.7 us (13%)
  other arithmetic  25.9 us (9%)
  local copies, waits for them, and re-layouts  17.4 us (6%)
  between operations  15.7 us (6%)
  starting transfers between devices  10.8 us (4%)
    ppermute x8, waiting for transfers between devices, body(): fars = [lax.ppermute(chip, 'aux', ACROSS) for chip in chips]  74.9 us
    dot_general x8, matrix products, body(): lax.dot_general(source[:, low:high], second, (((0,), (0,)), ((), ())), pr...  35.7 us
    pallas_call x1, Pallas kernels, gamma_of(): pl.pallas_call(gamma_kernel, grid=(naux // block,), in_specs=[pl.BlockSpe...  28.5 us
    pallas_call x1, Pallas kernels, split_orbitals(): pl.pallas_call(split_kernel, grid=(naux // block,), in_specs=[pl.BlockSpe...  24.9 us
    dynamic_update_slice x8, other arithmetic, body(): amplitude = lax.dynamic_update_slice_in_dim(amplitude, amp, start, 0)  16.2 us
    reduce_scatter x1, waiting for transfers between devices, body(): lax.psum_scatter(density_part, 'occ', scatter_dimension=1, tiled=True)  15.8 us
    ppermute x8, waiting for transfers between devices, body(): amp_other = lax.ppermute(amp, 'aux', SIBLING)  14.1 us
    pallas_call x1, Pallas kernels, tilde_density(): pl.pallas_call(tilde_kernel, grid_spec=pltpu.PrefetchScalarGridSpec(num_s...  13.3 us
  transfers between devices with their start and end apart: 25, of which 16 were waited for; matrix products, arithmetic and copies ran while one was open for 15% of the time, Pallas kernels for 10%

profile of v3, /device:TPU:0, one launch (start us, length us, event | category | flops | bytes accessed | tf_op | source)
XLA Modules:
  0.0 276.9 jit_solution(4983158665136616791)
XLA Ops:
  7.2 24.9 %shard_map.71 = (bf16[2560,2048]{1,0:T(8,128)(2,1)}, bf16[2560,2048]{1,0:T(8,128)(2,1)}) custom-call(bf16[2560,1,2,2048]{3,2,1,0:T(2,128)(2,1)} %x_ref.1), custom_call_target="tpu_custom_call" | custom-call | tf_op jit(solution)/shard_map/pallas_call | solution.py:73
  32.1 7.4 %convolution_convert_fusion.7 = bf16[256,2048]{1,0:T(8,128)(2,1)S(1)} fusion(bf16[2560,2048]{1,0:T(8,128)(2,1)} %get-tuple-element.26.second_ref, bf16[2560,2048]{1,0:T(8,128)(2,1)} %get-tuple-element.39), kind=kOutput, calls=%fused_computation.7 | convolution fusion | flops 2684878848 | bytes 12845056 | tf_op jit(solution)/shard_map/dot_general | solution.py:173
  40.9 4.2 %convolution_convert_fusion.6 = bf16[256,2048]{1,0:T(8,128)(2,1)S(1)} fusion(bf16[2560,2048]{1,0:T(8,128)(2,1)S(1)} %copy-done, bf16[2560,2048]{1,0:T(8,128)(2,1)} %get-tuple-element.39), kind=kOutput, calls=%fused_computation.6 | convolution fusion | flops 2684878848 | bytes 12845056 | tf_op jit(solution)/shard_map/dot_general | solution.py:173
  46.9 7.8 %convolution_convert_fusion.5 = bf16[256,2048]{1,0:T(8,128)(2,1)S(1)} fusion(bf16[2560,2048]{1,0:T(8,128)(2,1)} %get-tuple-element.26.second_ref, bf16[2560,2048]{1,0:T(8,128)(2,1)} %get-tuple-element.39), kind=kOutput, calls=%fused_computation.5 | convolution fusion | flops 2684878848 | bytes 12845056 | tf_op jit(solution)/shard_map/dot_general | solution.py:173
  56.3 4.5 %convolution_convert_fusion.4 = bf16[256,2048]{1,0:T(8,128)(2,1)S(1)} fusion(bf16[2560,2048]{1,0:T(8,128)(2,1)S(1)} %bitcast.34, bf16[2560,2048]{1,0:T(8,128)(2,1)} %get-tuple-element.39), kind=kOutput, calls=%fused_computation.4 | convolution fusion | flops 2684878848 | bytes 12845056 | tf_op jit(solution)/shard_map/dot_general | solution.py:173
  60.9 3.0 %collective-permute-start.3 = (bf16[128,2048]{1,0:T(8,128)(2,1)}, bf16[128,2048]{1,0:T(8,128)(2,1)}, u32[]{:S(2)}, u32[]{:S(2)}) collective-permute-start(bf16[128,2048]{1,0:T(8,128)(2,1)} %add_convert_fusion.6), channel_id=1, source_target_pairs={{0,8},{8,0},{4,12},{12,4},{1,9},{9,1},{5,13},{13,5},{2,10},{10,2},... | collective-permute-start | bytes 1572872 | tf_op jit(solution)/shard_map/ppermute | solution.py:183
  64.9 2.9 %convolution_convert_fusion.3 = bf16[256,2048]{1,0:T(8,128)(2,1)S(1)} fusion(bf16[2560,2048]{1,0:T(8,128)(2,1)S(1)} %bitcast.34, bf16[2560,2048]{1,0:T(8,128)(2,1)S(1)} %bitcast.36), kind=kOutput, calls=%fused_computation.3 | convolution fusion | flops 2684878848 | bytes 12845056 | tf_op jit(solution)/shard_map/dot_general | solution.py:173
  68.8 3.1 %convolution_convert_fusion.2 = bf16[256,2048]{1,0:T(8,128)(2,1)S(1)} fusion(bf16[2560,2048]{1,0:T(8,128)(2,1)S(1)} %bitcast.34, bf16[2560,2048]{1,0:T(8,128)(2,1)S(1)} %bitcast.36), kind=kOutput, calls=%fused_computation.2 | convolution fusion | flops 2684878848 | bytes 12845056 | tf_op jit(solution)/shard_map/dot_general | solution.py:173
  72.7 2.9 %convolution_convert_fusion.1 = bf16[256,2048]{1,0:T(8,128)(2,1)S(1)} fusion(bf16[2560,2048]{1,0:T(8,128)(2,1)S(1)} %bitcast.34, bf16[2560,2048]{1,0:T(8,128)(2,1)S(1)} %bitcast.36), kind=kOutput, calls=%fused_computation.1 | convolution fusion | flops 2684878848 | bytes 12845056 | tf_op jit(solution)/shard_map/dot_general | solution.py:173
  75.8 2.9 %convolution_convert_fusion = bf16[256,2048]{1,0:T(8,128)(2,1)S(1)} fusion(bf16[2560,2048]{1,0:T(8,128)(2,1)S(1)} %bitcast.34, bf16[2560,2048]{1,0:T(8,128)(2,1)S(1)} %bitcast.36), kind=kOutput, calls=%fused_computation | convolution fusion | flops 2684878848 | bytes 12845056 | tf_op jit(solution)/shard_map/dot_general | solution.py:173
  83.6 2.0 collective-permute-start.7
  87.7 2.0 add_convert_fusion
  90.9 7.7 %collective-permute-done.1 = bf16[128,2048]{1,0:T(8,128)(2,1)S(1)} collective-permute-done((bf16[128,2048]{1,0:T(8,128)(2,1)}, bf16[128,2048]{1,0:T(8,128)(2,1)S(1)}, u32[]{:S(2)}, u32[]{:S(2)}) %collective-permute-start.1) | collective-permute-done | bytes 524320 | tf_op jit(solution)/shard_map/ppermute | solution.py:183
  98.5 11.2 %collective-permute-done.7 = bf16[128,2048]{1,0:T(8,128)(2,1)S(1)} collective-permute-done((bf16[128,2048]{1,0:T(8,128)(2,1)}, bf16[128,2048]{1,0:T(8,128)(2,1)S(1)}, u32[]{:S(2)}, u32[]{:S(2)}) %collective-permute-start.7) | collective-permute-done | bytes 524320 | tf_op jit(solution)/shard_map/ppermute | solution.py:183
  109.8 11.2 %collective-permute-done.5 = bf16[128,2048]{1,0:T(8,128)(2,1)S(1)} collective-permute-done((bf16[128,2048]{1,0:T(8,128)(2,1)}, bf16[128,2048]{1,0:T(8,128)(2,1)S(1)}, u32[]{:S(2)}, u32[]{:S(2)}) %collective-permute-start.5) | collective-permute-done | bytes 524320 | tf_op jit(solution)/shard_map/ppermute | solution.py:183
  121.0 11.2 %collective-permute-done.11 = bf16[128,2048]{1,0:T(8,128)(2,1)S(1)} collective-permute-done((bf16[128,2048]{1,0:T(8,128)(2,1)S(1)}, bf16[128,2048]{1,0:T(8,128)(2,1)S(1)}, u32[]{:S(2)}, u32[]{:S(2)}) %collective-permute-start.11) | collective-permute-done | bytes 524320 | tf_op jit(solution)/shard_map/ppermute | solution.py:183
  132.2 10.3 %collective-permute-done.9 = bf16[128,2048]{1,0:T(8,128)(2,1)S(1)} collective-permute-done((bf16[128,2048]{1,0:T(8,128)(2,1)S(1)}, bf16[128,2048]{1,0:T(8,128)(2,1)S(1)}, u32[]{:S(2)}, u32[]{:S(2)}) %collective-permute-start.9) | collective-permute-done | bytes 524320 | tf_op jit(solution)/shard_map/ppermute | solution.py:183
  142.6 4.5 %broadcast_in_dim.20 = bf16[2048,2048]{1,0:T(8,128)(2,1)} broadcast(bf16[]{:T(256)} %constant.43.clone.1), dimensions={} | broadcast | bytes 8388610 | tf_op jit(solution)/shard_map/broadcast_in_dim | solution.py:186
  148.6 2.1 collective-permute-done.14
  151.5 2.6 constant_dynamic-update-slice_fusion.13
  154.3 2.1 collective-permute-done.15
  158.3 2.5 constant_dynamic-update-slice_fusion.11
  160.9 2.0 collective-permute-done.16
  163.7 2.3 constant_dynamic-update-slice_fusion.9
  168.8 2.3 constant_dynamic-update-slice_fusion.7
  173.8 2.3 constant_dynamic-update-slice_fusion.5
  178.9 11.6 %collective-permute-done.20 = bf16[128,2048]{1,0:T(8,128)(2,1)S(1)} collective-permute-done((bf16[128,2048]{1,0:T(8,128)(2,1)S(1)}, bf16[128,2048]{1,0:T(8,128)(2,1)S(1)}, u32[]{:S(2)}, u32[]{:S(2)}) %collective-permute-start.20) | collective-permute-done | bytes 524320 | tf_op jit(solution)/shard_map/ppermute | solution.py:183
  194.7 11.6 %collective-permute-done.22 = bf16[128,2048]{1,0:T(8,128)(2,1)S(1)} collective-permute-done((bf16[128,2048]{1,0:T(8,128)(2,1)S(1)}, bf16[128,2048]{1,0:T(8,128)(2,1)S(1)}, u32[]{:S(2)}, u32[]{:S(2)}) %collective-permute-start.22) | collective-permute-done | bytes 524320 | tf_op jit(solution)/shard_map/ppermute | solution.py:183
  210.3 13.3 %shard_map.72 = (bf16[2048,2048]{1,0:T(8,128)(2,1)}, bf16[512,2048]{1,0:T(8,128)(2,1)}) custom-call(s32[1]{0:T(128)} %bitcast.me_ref, bf16[2048,2048]{1,0:T(8,128)(2,1)} %constant_dynamic-update-slice_fusion.own_ref.rows_ref.cols_ref, bf16[2048,2048]{1,0:T(8,128)(2,1)} %constant_dynamic-update-slice_fusion.own_ref.rows_ref.cols_ref, ...), custom_call_target="tpu_custom_call" | custom-call | tf_op jit(solution)/shard_map/pallas_call | solution.py:101
  223.6 28.5 %shard_map.73 = bf16[2560,2048]{1,0:T(8,128)(2,1)} custom-call(bf16[2560,2048]{1,0:T(8,128)(2,1)} %get-tuple-element.26.second_ref, bf16[2048,2048]{1,0:T(8,128)(2,1)} %get-tuple-element.48.tilde_ref), custom_call_target="tpu_custom_call" | custom-call | flops 21474836480 | bytes 29360128 | tf_op jit(solution)/shard_map/pallas_call | solution.py:137
  252.1 15.8 %reduce-scatter.2.cloned.1.call-done = bf16[512,512]{1,0:T(8,128)(2,1)} async-done(((bf16[512,2048]{1,0:T(8,128)(2,1)}), bf16[512,512]{1,0:T(8,128)(2,1)}) %reduce-scatter.2.cloned.1.call-update) | async-done | bytes 524304 | tf_op jit(solution)/shard_map/reduce_scatter | solution.py:200
  267.9 2.1 convert_element_type.234
  (115 shorter events, 36.3 us)
Async XLA Ops:
  7.2 260.7 %reduce-scatter.2.cloned.1.call-start = ((), (), s32[]{:S(2)}) async-start(), calls=%async_computation.1 | async-start | bytes 2621440 | tf_op jit(solution)/shard_map/reduce_scatter | solution.py:200
  40.4 5.6 %collective-permute-start = (bf16[128,2048]{1,0:T(8,128)(2,1)}, bf16[128,2048]{1,0:T(8,128)(2,1)S(1)}, u32[]{:S(2)}, u32[]{:S(2)}) collective-permute-start(bf16[128,2048]{1,0:T(8,128)(2,1)} %constant_dynamic-slice_fusion.15), channel_id=1, source_target_pairs={{0,4},{4,0},{8,12},{12,8},{1,5},{5,1},{9,13},{13,9},{2,6},{6,2},{1... | collective-permute-start | bytes 1572872 | tf_op jit(solution)/shard_map/ppermute | solution.py:181
  45.9 8.8 %collective-permute-start.2 = (bf16[128,2048]{1,0:T(8,128)(2,1)}, bf16[128,2048]{1,0:T(8,128)(2,1)S(1)}, u32[]{:S(2)}, u32[]{:S(2)}) collective-permute-start(bf16[128,2048]{1,0:T(8,128)(2,1)} %constant_dynamic-slice_fusion.14), channel_id=1, source_target_pairs={{0,4},{4,0},{8,12},{12,8},{1,5},{5,1},{9,13},{13,9},{2,6},{6,2},{1... | collective-permute-start | bytes 1572872 | tf_op jit(solution)/shard_map/ppermute | solution.py:181
  55.7 8.2 %collective-permute-start.4 = (bf16[128,2048]{1,0:T(8,128)(2,1)S(1)}, bf16[128,2048]{1,0:T(8,128)(2,1)S(1)}, u32[]{:S(2)}, u32[]{:S(2)}) collective-permute-start(bf16[128,2048]{1,0:T(8,128)(2,1)S(1)} %constant_dynamic-slice_fusion.13), channel_id=1, source_target_pairs={{0,4},{4,0},{8,12},{12,8},{1,5},{5,1},{9,13},{13,9},{2,6},{6,2},{1... | collective-permute-start | bytes 1572872 | tf_op jit(solution)/shard_map/ppermute | solution.py:181
  60.8 6.9 %collective-permute-start.6 = (bf16[128,2048]{1,0:T(8,128)(2,1)S(1)}, bf16[128,2048]{1,0:T(8,128)(2,1)S(1)}, u32[]{:S(2)}, u32[]{:S(2)}) collective-permute-start(bf16[128,2048]{1,0:T(8,128)(2,1)S(1)} %constant_dynamic-slice_fusion.12), channel_id=1, source_target_pairs={{0,4},{4,0},{8,12},{12,8},{1,5},{5,1},{9,13},{13,9},{2,6},{6,2},{1... | collective-permute-start | bytes 1572872 | tf_op jit(solution)/shard_map/ppermute | solution.py:181
  60.9 24.7 %collective-permute-start.3 = (bf16[128,2048]{1,0:T(8,128)(2,1)}, bf16[128,2048]{1,0:T(8,128)(2,1)}, u32[]{:S(2)}, u32[]{:S(2)}) collective-permute-start(bf16[128,2048]{1,0:T(8,128)(2,1)} %add_convert_fusion.6), channel_id=1, source_target_pairs={{0,8},{8,0},{4,12},{12,4},{1,9},{9,1},{5,13},{13,5},{2,10},{10,2},... | collective-permute-start | bytes 1572872 | tf_op jit(solution)/shard_map/ppermute | solution.py:183
  68.8 3.8 %collective-permute-start.8 = (bf16[128,2048]{1,0:T(8,128)(2,1)S(1)}, bf16[128,2048]{1,0:T(8,128)(2,1)S(1)}, u32[]{:S(2)}, u32[]{:S(2)}) collective-permute-start(bf16[128,2048]{1,0:T(8,128)(2,1)S(1)} %constant_dynamic-slice_fusion.11), channel_id=1, source_target_pairs={{0,4},{4,0},{8,12},{12,8},{1,5},{5,1},{9,13},{13,9},{2,6},{6,2},{1... | collective-permute-start | bytes 1572872 | tf_op jit(solution)/shard_map/ppermute | solution.py:181
  72.0 3.6 %collective-permute-start.10 = (bf16[128,2048]{1,0:T(8,128)(2,1)S(1)}, bf16[128,2048]{1,0:T(8,128)(2,1)S(1)}, u32[]{:S(2)}, u32[]{:S(2)}) collective-permute-start(bf16[128,2048]{1,0:T(8,128)(2,1)S(1)} %constant_dynamic-slice_fusion.10), channel_id=1, source_target_pairs={{0,4},{4,0},{8,12},{12,8},{1,5},{5,1},{9,13},{13,9},{2,6},{6,2},{1... | collective-permute-start | bytes 1572872 | tf_op jit(solution)/shard_map/ppermute | solution.py:181
  79.5 6.1 %collective-permute-start.13 = (bf16[128,2048]{1,0:T(8,128)(2,1)}, bf16[128,2048]{1,0:T(8,128)(2,1)}, u32[]{:S(2)}, u32[]{:S(2)}) collective-permute-start(bf16[128,2048]{1,0:T(8,128)(2,1)} %constant_dynamic-slice_fusion.8), channel_id=1, source_target_pairs={{0,4},{4,0},{8,12},{12,8},{1,5},{5,1},{9,13},{13,9},{2,6},{6,2},{1... | collective-permute-start | bytes 1572872 | tf_op jit(solution)/shard_map/ppermute | solution.py:181
  80.4 7.2 %collective-permute-start.12 = (bf16[128,2048]{1,0:T(8,128)(2,1)}, bf16[128,2048]{1,0:T(8,128)(2,1)}, u32[]{:S(2)}, u32[]{:S(2)}) collective-permute-start(bf16[128,2048]{1,0:T(8,128)(2,1)} %constant_dynamic-slice_fusion.9), channel_id=1, source_target_pairs={{0,4},{4,0},{8,12},{12,8},{1,5},{5,1},{9,13},{13,9},{2,6},{6,2},{1... | collective-permute-start | bytes 1572872 | tf_op jit(solution)/shard_map/ppermute | solution.py:181
  81.1 65.9 %copy-start.4 = (bf16[128,2048]{1,0:T(8,128)(2,1)S(1)}, bf16[128,2048]{1,0:T(8,128)(2,1)}, u32[]{:S(2)}) copy-start(bf16[128,2048]{1,0:T(8,128)(2,1)} %add_convert_fusion.7) | copy-start | bytes 1572868
  83.5 15.1 %collective-permute-start.1 = (bf16[128,2048]{1,0:T(8,128)(2,1)}, bf16[128,2048]{1,0:T(8,128)(2,1)S(1)}, u32[]{:S(2)}, u32[]{:S(2)}) collective-permute-start(bf16[128,2048]{1,0:T(8,128)(2,1)} %add_convert_fusion.7), channel_id=1, source_target_pairs={{0,8},{8,0},{4,12},{12,4},{1,9},{9,1},{5,13},{13,5},{2,10},{10,2},... | collective-permute-start | bytes 1572872 | tf_op jit(solution)/shard_map/ppermute | solution.py:183
  83.6 26.2 %collective-permute-start.7 = (bf16[128,2048]{1,0:T(8,128)(2,1)}, bf16[128,2048]{1,0:T(8,128)(2,1)S(1)}, u32[]{:S(2)}, u32[]{:S(2)}) collective-permute-start(bf16[128,2048]{1,0:T(8,128)(2,1)} %add_convert_fusion.4), channel_id=1, source_target_pairs={{0,8},{8,0},{4,12},{12,4},{1,9},{9,1},{5,13},{13,5},{2,10},{10,2},... | collective-permute-start | bytes 1572872 | tf_op jit(solution)/shard_map/ppermute | solution.py:183
  85.6 35.4 %collective-permute-start.5 = (bf16[128,2048]{1,0:T(8,128)(2,1)}, bf16[128,2048]{1,0:T(8,128)(2,1)S(1)}, u32[]{:S(2)}, u32[]{:S(2)}) collective-permute-start(bf16[128,2048]{1,0:T(8,128)(2,1)} %add_convert_fusion.5), channel_id=1, source_target_pairs={{0,8},{8,0},{4,12},{12,4},{1,9},{9,1},{5,13},{13,5},{2,10},{10,2},... | collective-permute-start | bytes 1572872 | tf_op jit(solution)/shard_map/ppermute | solution.py:183
  85.7 46.6 %collective-permute-start.11 = (bf16[128,2048]{1,0:T(8,128)(2,1)S(1)}, bf16[128,2048]{1,0:T(8,128)(2,1)S(1)}, u32[]{:S(2)}, u32[]{:S(2)}) collective-permute-start(bf16[128,2048]{1,0:T(8,128)(2,1)S(1)} %add_convert_fusion.2), channel_id=1, source_target_pairs={{0,8},{8,0},{4,12},{12,4},{1,9},{9,1},{5,13},{13,5},{2,10},{10,2},... | collective-permute-start | bytes 1572872 | tf_op jit(solution)/shard_map/ppermute | solution.py:183
  87.6 54.9 %collective-permute-start.9 = (bf16[128,2048]{1,0:T(8,128)(2,1)S(1)}, bf16[128,2048]{1,0:T(8,128)(2,1)S(1)}, u32[]{:S(2)}, u32[]{:S(2)}) collective-permute-start(bf16[128,2048]{1,0:T(8,128)(2,1)S(1)} %add_convert_fusion.3), channel_id=1, source_target_pairs={{0,8},{8,0},{4,12},{12,4},{1,9},{9,1},{5,13},{13,5},{2,10},{10,2},... | collective-permute-start | bytes 1572872 | tf_op jit(solution)/shard_map/ppermute | solution.py:183
  89.7 68.6 %copy-start.2 = (bf16[128,2048]{1,0:T(8,128)(2,1)S(1)}, bf16[128,2048]{1,0:T(8,128)(2,1)}, u32[]{:S(2)}) copy-start(bf16[128,2048]{1,0:T(8,128)(2,1)} %add_convert_fusion.5) | copy-start | bytes 1572868
  109.8 38.7 %copy-start.8 = (bf16[128,2048]{1,0:T(8,128)(2,1)}, bf16[128,2048]{1,0:T(8,128)(2,1)S(1)}, u32[]{:S(2)}) copy-start(bf16[128,2048]{1,0:T(8,128)(2,1)S(1)} %collective-permute-done.7) | copy-start | bytes 1572868
  121.0 27.5 %copy-start.9 = (bf16[128,2048]{1,0:T(8,128)(2,1)}, bf16[128,2048]{1,0:T(8,128)(2,1)S(1)}, u32[]{:S(2)}) copy-start(bf16[128,2048]{1,0:T(8,128)(2,1)S(1)} %collective-permute-done.5) | copy-start | bytes 1572868
  132.2 16.2 %copy-start.6 = (bf16[128,2048]{1,0:T(8,128)(2,1)}, bf16[128,2048]{1,0:T(8,128)(2,1)S(1)}, u32[]{:S(2)}) copy-start(bf16[128,2048]{1,0:T(8,128)(2,1)S(1)} %collective-permute-done.11) | copy-start | bytes 1572868
  142.5 21.2 %copy-start.1 = (bf16[128,2048]{1,0:T(8,128)(2,1)S(1)}, bf16[128,2048]{1,0:T(8,128)(2,1)}, u32[]{:S(2)}) copy-start(bf16[128,2048]{1,0:T(8,128)(2,1)} %add_convert_fusion.4) | copy-start | bytes 1572868
  148.5 2.2 collective-permute-start.14
  154.1 37.8 %copy-start.3 = (bf16[128,2048]{1,0:T(8,128)(2,1)S(1)}, bf16[128,2048]{1,0:T(8,128)(2,1)}, u32[]{:S(2)}) copy-start(bf16[128,2048]{1,0:T(8,128)(2,1)} %add_convert_fusion) | copy-start | bytes 1572868
  154.1 2.3 collective-permute-start.15
  160.8 2.1 collective-permute-start.16
  166.0 1.9 collective-permute-start.17
  171.1 1.9 collective-permute-start.18
  176.1 1.9 collective-permute-start.19
  176.3 14.2 %collective-permute-start.20 = (bf16[128,2048]{1,0:T(8,128)(2,1)S(1)}, bf16[128,2048]{1,0:T(8,128)(2,1)S(1)}, u32[]{:S(2)}, u32[]{:S(2)}) collective-permute-start(bf16[128,2048]{1,0:T(8,128)(2,1)S(1)} %add_convert_fusion.1), channel_id=1, source_target_pairs={{0,8},{8,0},{4,12},{12,4},{1,9},{9,1},{5,13},{13,5},{2,10},{10,2},... | collective-permute-start | bytes 1572872 | tf_op jit(solution)/shard_map/ppermute | solution.py:183
  191.9 1.9 collective-permute-start.21
  191.9 14.3 %collective-permute-start.22 = (bf16[128,2048]{1,0:T(8,128)(2,1)S(1)}, bf16[128,2048]{1,0:T(8,128)(2,1)S(1)}, u32[]{:S(2)}, u32[]{:S(2)}) collective-permute-start(bf16[128,2048]{1,0:T(8,128)(2,1)S(1)} %copy-done.3), channel_id=1, source_target_pairs={{0,8},{8,0},{4,12},{12,4},{1,9},{9,1},{5,13},{13,5},{2,10},{10,2},... | collective-permute-start | bytes 1572872 | tf_op jit(solution)/shard_map/ppermute | solution.py:183
  207.5 1.9 collective-permute-start.23
  (12 other events, 95.2 us)
Sparse Core Ops, SparseCore 0:
  223.7 44.1 reduce-scatter.1
